TPU v7x, 768 devices: a whole 4x8x12 slice. The times are simulated.
768 devices in a mesh: dp: 192 (over z, y_lo, x), rows: 4 (over y_hi, core).
Axes of the slice: x: 4, y: 8 (y_hi: 2, y_lo: 4; y = y_hi * 4 + y_lo), z: 12, core: 2. Of those that a mesh axis runs over, the one named last changes fastest.
Arguments:
- images: bfloat16 [98304, 1152], P(('dp', 'rows')), may hold values from -5 to 5
- texts: bfloat16 [98304, 1152], P(('dp', 'rows')), may hold values from -5 to 5
- positive_offset: int32 [98304], P(('dp', 'rows')), may hold values from 0 to 5
- logit_log_scale: float32 [1], replicated, may hold values from 1.6 to 2.6
- bias: float32 [1], replicated, may hold values from -4 to -2
Outputs:
- image_gradient: float32 [98304, 1152], P(('dp', 'rows'))
- text_gradient: float32 [98304, 1152], P(('dp', 'rows'))
All inputs are finite; a program needn't handle non-finite values.
Results may differ from a plain program's by a relative error of at most 0.004.
Values may be sent and summed in bfloat16 or wider, within the bound.
No kernel may reach another device: no remote copies, remote signals or barrier semaphores. Data moves between devices by JAX's collectives and lax.ppermute only.
A program may use at most 32 MiB of HBM per device.

v0:
```python
import jax
import jax.numpy as jnp
from jax import lax
from jax.sharding import PartitionSpec as P

STEPS = 6


def shifted(block, axis, distance):
    devices = range(lax.axis_size(axis))
    route = [((i - distance) % len(devices), i) for i in devices]
    return lax.ppermute(block, axis, route)


def unit_rows(values):
    widened = values.astype(jnp.float32)
    row_norm = jnp.sqrt(jnp.sum(widened * widened, axis=1, keepdims=True) + 1e-06)
    return (widened / row_norm, row_norm)


def project_tangent(unit_values, row_norm, direction):
    inner = jnp.sum(unit_values * direction, axis=1, keepdims=True)
    return (direction - unit_values * inner) / row_norm


def send_home(text_portion, offset):
    return shifted(text_portion, "dp", offset)


def local(images, texts, positive_offset, logit_log_scale, bias):
    unit_image_rows, image_norm_values = unit_rows(images)
    unit_text_rows, text_norm_values = unit_rows(texts)
    image_low = unit_image_rows.astype(jnp.bfloat16)
    text_low = unit_text_rows.astype(jnp.bfloat16)
    group_image, group_offset = (
        lax.all_gather(image_low, "rows", axis=0, tiled=True),
        lax.all_gather(positive_offset, "rows", axis=0, tiled=True),
    )
    logit_scale_value = jnp.exp(logit_log_scale[0])
    logit_bias = bias[0]
    quarter = texts.shape[0]
    group_rows = group_image.shape[0]
    half_window = STEPS // 2
    target = group_offset - (half_window - 1)
    lane_index = lax.axis_index("rows")
    same_index = (
        jnp.arange(group_rows)[:, None] == lane_index * quarter + jnp.arange(quarter)[None, :]
    )

    def contribute(paired_side, offset, image_total_sum):
        pair_scores = lax.dot_general(
            group_image, paired_side, (((1,), (1,)), ((), ())), preferred_element_type=jnp.float32
        )
        pair_logits = logit_scale_value * pair_scores + logit_bias
        positive = jnp.logical_and(target[:, None] == offset, same_index)
        label_sign = jnp.where(positive, 1.0, -1.0).astype(jnp.float32)
        pair_weights = (-label_sign * jax.nn.sigmoid(-label_sign * pair_logits)).astype(
            jnp.bfloat16
        )
        image_total_sum = image_total_sum + jnp.dot(
            pair_weights, paired_side, preferred_element_type=jnp.float32
        )
        text_portion = lax.dot_general(
            pair_weights, group_image, (((0,), (0,)), ((), ())), preferred_element_type=jnp.float32
        )
        return (image_total_sum, text_portion)

    initial = jnp.zeros((group_rows, images.shape[1]), jnp.float32)
    paired_side = shifted(text_low, "dp", -half_window)
    image_total_sum, text_portion = contribute(paired_side, half_window, initial)
    text_total_sum = send_home(text_portion, half_window)
    for offset in range(half_window - 1, -half_window, -1):
        paired_side = shifted(paired_side, "dp", 1)
        image_total_sum, text_portion = contribute(paired_side, offset, image_total_sum)
        if offset == 0:
            text_total_sum = text_total_sum + text_portion
        else:
            text_total_sum = text_total_sum + send_home(text_portion, offset)
    local_sum = lax.psum_scatter(image_total_sum, "rows", scatter_dimension=0, tiled=True)
    image_gradient = project_tangent(
        unit_image_rows, image_norm_values, logit_scale_value * local_sum
    )
    text_gradient = project_tangent(
        unit_text_rows, text_norm_values, logit_scale_value * text_total_sum
    )
    return (image_gradient, text_gradient)


def solution(mesh):
    return jax.shard_map(
        local,
        mesh=mesh,
        in_specs=(P(("dp", "rows"), None), P(("dp", "rows"), None), P(("dp", "rows")), P(), P()),
        out_specs=(P(("dp", "rows"), None), P(("dp", "rows"), None)),
        check_vma=False,
    )
```

profile of v0, /device:TPU:15, one launch (start us, length us, event | category | flops | bytes accessed | tf_op | source)
XLA Modules:
  0.0 207.9 jit_solution(9804780703379349342)
XLA Ops:
  7.2 0.0 copy-start.1
  7.2 0.0 copy-start.4
  7.2 0.0 all-gather.3.cloned.1.call-start
  7.2 1.1 fusion.48
  8.4 1.8 fusion.56
  10.2 0.0 all-gather.3.cloned.1.call-update
  10.2 0.0 reduce-scatter.2.cloned.1.call-start
  10.3 0.0 copy-done.1
  10.3 0.1 fusion.49
  10.4 0.1 fusion.57
  10.6 2.1 %collective-permute-start = (bf16[128,1152]{1,0:T(8,128)(2,1)S(1)}, bf16[128,1152]{1,0:T(8,128)(2,1)S(1)}, u32[]{:S(2)}, u32[]{:S(2)}) collective-permute-start(bf16[128,1152]{1,0:T(8,128)(2,1)S(1)} %fusion.57), channel_id=1, source_target_pairs={{12,0},{16,4},{20,8},{24,12},{28,16},{32,20},{36,24},{40,28},{44,3... | collective-permute-start | bytes 884744 | tf_op jit(solution)/shard_map/ppermute | solution.py:12
  12.7 8.6 %collective-permute-done = bf16[128,1152]{1,0:T(8,128)(2,1)S(1)} collective-permute-done((bf16[128,1152]{1,0:T(8,128)(2,1)S(1)}, bf16[128,1152]{1,0:T(8,128)(2,1)S(1)}, u32[]{:S(2)}, u32[]{:S(2)}) %collective-permute-start) | collective-permute-done | bytes 294944 | tf_op jit(solution)/shard_map/ppermute | solution.py:12
  21.2 3.4 %collective-permute-start.1 = (bf16[128,1152]{1,0:T(8,128)(2,1)S(1)}, bf16[128,1152]{1,0:T(8,128)(2,1)S(1)}, u32[]{:S(2)}, u32[]{:S(2)}) collective-permute-start(bf16[128,1152]{1,0:T(8,128)(2,1)S(1)} %collective-permute-done), channel_id=1, source_target_pairs={{764,0},{0,4},{4,8},{8,12},{12,16},{16,20},{20,24},{24,28},{28,32}... | collective-permute-start | bytes 884744 | tf_op jit(solution)/shard_map/ppermute | solution.py:12
  24.7 5.4 %collective-permute-done.1 = bf16[128,1152]{1,0:T(8,128)(2,1)S(1)} collective-permute-done((bf16[128,1152]{1,0:T(8,128)(2,1)S(1)}, bf16[128,1152]{1,0:T(8,128)(2,1)S(1)}, u32[]{:S(2)}, u32[]{:S(2)}) %collective-permute-start.1) | collective-permute-done | bytes 294944 | tf_op jit(solution)/shard_map/ppermute | solution.py:12
  30.1 5.5 %collective-permute-start.2 = (bf16[128,1152]{1,0:T(8,128)(2,1)S(1)}, bf16[128,1152]{1,0:T(8,128)(2,1)S(1)}, u32[]{:S(2)}, u32[]{:S(2)}) collective-permute-start(bf16[128,1152]{1,0:T(8,128)(2,1)S(1)} %collective-permute-done.1), channel_id=1, source_target_pairs={{764,0},{0,4},{4,8},{8,12},{12,16},{16,20},{20,24},{24,28},{28,32}... | collective-permute-start | bytes 884744 | tf_op jit(solution)/shard_map/ppermute | solution.py:12
  35.6 15.9 %collective-permute-done.2 = bf16[128,1152]{1,0:T(8,128)(2,1)S(1)} collective-permute-done((bf16[128,1152]{1,0:T(8,128)(2,1)S(1)}, bf16[128,1152]{1,0:T(8,128)(2,1)S(1)}, u32[]{:S(2)}, u32[]{:S(2)}) %collective-permute-start.2) | collective-permute-done | bytes 294944 | tf_op jit(solution)/shard_map/ppermute | solution.py:12
  51.5 6.7 %collective-permute-start.3 = (bf16[128,1152]{1,0:T(8,128)(2,1)S(1)}, bf16[128,1152]{1,0:T(8,128)(2,1)S(1)}, u32[]{:S(2)}, u32[]{:S(2)}) collective-permute-start(bf16[128,1152]{1,0:T(8,128)(2,1)S(1)} %collective-permute-done.2), channel_id=1, source_target_pairs={{764,0},{0,4},{4,8},{8,12},{12,16},{16,20},{20,24},{24,28},{28,32}... | collective-permute-start | bytes 884744 | tf_op jit(solution)/shard_map/ppermute | solution.py:12
  58.2 5.4 %collective-permute-done.3 = bf16[128,1152]{1,0:T(8,128)(2,1)S(1)} collective-permute-done((bf16[128,1152]{1,0:T(8,128)(2,1)S(1)}, bf16[128,1152]{1,0:T(8,128)(2,1)S(1)}, u32[]{:S(2)}, u32[]{:S(2)}) %collective-permute-start.3) | collective-permute-done | bytes 294944 | tf_op jit(solution)/shard_map/ppermute | solution.py:12
  63.7 6.2 %collective-permute-start.4 = (bf16[128,1152]{1,0:T(8,128)(2,1)S(1)}, bf16[128,1152]{1,0:T(8,128)(2,1)S(1)}, u32[]{:S(2)}, u32[]{:S(2)}) collective-permute-start(bf16[128,1152]{1,0:T(8,128)(2,1)S(1)} %collective-permute-done.3), channel_id=1, source_target_pairs={{764,0},{0,4},{4,8},{8,12},{12,16},{16,20},{20,24},{24,28},{28,32}... | collective-permute-start | bytes 884744 | tf_op jit(solution)/shard_map/ppermute | solution.py:12
  71.2 0.0 copy-done.4
  71.2 10.9 %all-gather = s32[4,1,128]{2,1,0:T(1,128)S(1)} all-gather(s32[1,1,128]{2,1,0:T(1,128)S(1)} %bitcast.51), channel_id=1, replica_groups=mesh['dp'=192,'rows'=4] {'rows'}, dimensions={0}, use_global_device_ids=true | all-gather | bytes 2560 | tf_op jit(solution)/shard_map/all_gather | solution.py:37
  82.1 0.0 collective-permute-done.4
  82.1 1.9 collective-permute-start.5
  84.1 0.0 all-gather.3.cloned.1.call-done
  84.1 1.8 fusion.47
  85.9 0.0 copy-start
  85.9 0.4 fusion.58
  86.4 0.8 copy-done
  87.2 0.5 fusion.46
  87.7 0.5 convolution_add_fusion.4
  88.2 0.5 fusion.45
  88.7 0.5 convolution_add_fusion.3
  89.2 0.5 fusion.44
  89.7 0.5 convolution_add_fusion.2
  90.2 0.5 fusion.43
  90.7 0.5 convolution_add_fusion.1
  91.2 1.3 collective-permute-done.5
  92.5 0.5 fusion.42
  93.0 1.9 convolution_add_fusion
  94.9 0.0 reduce-scatter.2.cloned.1.call-update
  94.9 0.4 fusion.63
  95.3 1.9 collective-permute-start.10
  97.2 0.4 fusion.62
  97.6 5.5 %collective-permute-start.9 = (f32[128,1152]{1,0:T(8,128)S(1)}, f32[128,1152]{1,0:T(8,128)S(1)}, u32[]{:S(2)}, u32[]{:S(2)}) collective-permute-start(f32[128,1152]{1,0:T(8,128)S(1)} %fusion.62), channel_id=1, source_target_pairs={{4,0},{8,4},{12,8},{16,12},{20,16},{24,20},{28,24},{32,28},{36,32}... | collective-permute-start | bytes 1769480 | tf_op jit(solution)/shard_map/ppermute | solution.py:12
  103.1 0.4 fusion.61
  103.5 1.9 collective-permute-start.8
  105.4 0.4 fusion.59
  105.8 3.8 %collective-permute-start.6 = (f32[128,1152]{1,0:T(8,128)S(1)}, f32[128,1152]{1,0:T(8,128)S(1)}, u32[]{:S(2)}, u32[]{:S(2)}) collective-permute-start(f32[128,1152]{1,0:T(8,128)S(1)} %fusion.59), channel_id=1, source_target_pairs={{756,0},{760,4},{764,8},{0,12},{4,16},{8,20},{12,24},{16,28},{20,3... | collective-permute-start | bytes 1769480 | tf_op jit(solution)/shard_map/ppermute | solution.py:12
  109.6 0.4 fusion.60
  109.9 6.4 %collective-permute-start.7 = (f32[128,1152]{1,0:T(8,128)S(1)}, f32[128,1152]{1,0:T(8,128)S(1)}, u32[]{:S(2)}, u32[]{:S(2)}) collective-permute-start(f32[128,1152]{1,0:T(8,128)S(1)} %fusion.60), channel_id=1, source_target_pairs={{760,0},{764,4},{0,8},{4,12},{8,16},{12,20},{16,24},{20,28},{24,32... | collective-permute-start | bytes 1769480 | tf_op jit(solution)/shard_map/ppermute | solution.py:12
  116.3 0.0 collective-permute-done.10
  116.3 10.4 %collective-permute-done.9 = f32[128,1152]{1,0:T(8,128)S(1)} collective-permute-done((f32[128,1152]{1,0:T(8,128)S(1)}, f32[128,1152]{1,0:T(8,128)S(1)}, u32[]{:S(2)}, u32[]{:S(2)}) %collective-permute-start.9) | collective-permute-done | bytes 589856 | tf_op jit(solution)/shard_map/ppermute | solution.py:12
  126.7 0.0 collective-permute-done.8
  126.7 11.7 %collective-permute-done.6 = f32[128,1152]{1,0:T(8,128)S(1)} collective-permute-done((f32[128,1152]{1,0:T(8,128)S(1)}, f32[128,1152]{1,0:T(8,128)S(1)}, u32[]{:S(2)}, u32[]{:S(2)}) %collective-permute-start.6) | collective-permute-done | bytes 589856 | tf_op jit(solution)/shard_map/ppermute | solution.py:12
  138.4 14.5 %collective-permute-done.7 = f32[128,1152]{1,0:T(8,128)S(1)} collective-permute-done((f32[128,1152]{1,0:T(8,128)S(1)}, f32[128,1152]{1,0:T(8,128)S(1)}, u32[]{:S(2)}, u32[]{:S(2)}) %collective-permute-start.7) | collective-permute-done | bytes 589856 | tf_op jit(solution)/shard_map/ppermute | solution.py:12
  152.9 0.5 multiply_reduce_fusion
  153.4 0.0 copy-start.2
  153.4 1.0 subtract_divide_fusion
  154.5 44.2 %reduce-scatter.2.cloned.1.call-done = f32[128,1152]{1,0:T(8,128)} async-done(((f32[512,1152]{1,0:T(8,128)}), f32[128,1152]{1,0:T(8,128)}) %reduce-scatter.2.cloned.1.call-update) | async-done | bytes 589840 | tf_op jit(solution)/shard_map/reduce_scatter | solution.py:79
  198.6 0.0 copy-done.2
  198.7 0.0 copy-start.3
  198.7 1.4 multiply_reduce_fusion.1
  200.0 0.0 copy-done.3
  200.0 1.0 subtract_divide_fusion.1
  (4 shorter events, 0.1 us)
Async XLA Ops:
  7.2 3.1 %copy-start.1 = (bf16[128,1152]{1,0:T(8,128)(2,1)S(1)}, bf16[128,1152]{1,0:T(8,128)(2,1)}, u32[]{:S(2)}) copy-start(bf16[128,1152]{1,0:T(8,128)(2,1)} %param.6) | copy-start | bytes 884740
  7.2 64.0 %copy-start.4 = (s32[128]{0:T(128)S(1)}, s32[128]{0:T(128)}, u32[]{:S(2)}) copy-start(s32[128]{0:T(128)} %param.7) | copy-start | bytes 1540
  7.2 76.9 %all-gather.3.cloned.1.call-start = ((), (), s32[]{:S(2)}) async-start(), calls=%async_computation.1 | async-start | bytes 1474560 | tf_op jit(solution)/shard_map/all_gather | solution.py:36
  10.2 188.4 %reduce-scatter.2.cloned.1.call-start = ((), (), s32[]{:S(2)}) async-start(), calls=%async_computation.2 | async-start | bytes 2949120 | tf_op jit(solution)/shard_map/reduce_scatter | solution.py:79
  10.6 10.7 %collective-permute-start = (bf16[128,1152]{1,0:T(8,128)(2,1)S(1)}, bf16[128,1152]{1,0:T(8,128)(2,1)S(1)}, u32[]{:S(2)}, u32[]{:S(2)}) collective-permute-start(bf16[128,1152]{1,0:T(8,128)(2,1)S(1)} %fusion.57), channel_id=1, source_target_pairs={{12,0},{16,4},{20,8},{24,12},{28,16},{32,20},{36,24},{40,28},{44,3... | collective-permute-start | bytes 884744 | tf_op jit(solution)/shard_map/ppermute | solution.py:12
  21.2 8.8 %collective-permute-start.1 = (bf16[128,1152]{1,0:T(8,128)(2,1)S(1)}, bf16[128,1152]{1,0:T(8,128)(2,1)S(1)}, u32[]{:S(2)}, u32[]{:S(2)}) collective-permute-start(bf16[128,1152]{1,0:T(8,128)(2,1)S(1)} %collective-permute-done), channel_id=1, source_target_pairs={{764,0},{0,4},{4,8},{8,12},{12,16},{16,20},{20,24},{24,28},{28,32}... | collective-permute-start | bytes 884744 | tf_op jit(solution)/shard_map/ppermute | solution.py:12
  30.1 21.5 %collective-permute-start.2 = (bf16[128,1152]{1,0:T(8,128)(2,1)S(1)}, bf16[128,1152]{1,0:T(8,128)(2,1)S(1)}, u32[]{:S(2)}, u32[]{:S(2)}) collective-permute-start(bf16[128,1152]{1,0:T(8,128)(2,1)S(1)} %collective-permute-done.1), channel_id=1, source_target_pairs={{764,0},{0,4},{4,8},{8,12},{12,16},{16,20},{20,24},{24,28},{28,32}... | collective-permute-start | bytes 884744 | tf_op jit(solution)/shard_map/ppermute | solution.py:12
  51.5 12.1 %collective-permute-start.3 = (bf16[128,1152]{1,0:T(8,128)(2,1)S(1)}, bf16[128,1152]{1,0:T(8,128)(2,1)S(1)}, u32[]{:S(2)}, u32[]{:S(2)}) collective-permute-start(bf16[128,1152]{1,0:T(8,128)(2,1)S(1)} %collective-permute-done.2), channel_id=1, source_target_pairs={{764,0},{0,4},{4,8},{8,12},{12,16},{16,20},{20,24},{24,28},{28,32}... | collective-permute-start | bytes 884744 | tf_op jit(solution)/shard_map/ppermute | solution.py:12
  63.7 18.5 %collective-permute-start.4 = (bf16[128,1152]{1,0:T(8,128)(2,1)S(1)}, bf16[128,1152]{1,0:T(8,128)(2,1)S(1)}, u32[]{:S(2)}, u32[]{:S(2)}) collective-permute-start(bf16[128,1152]{1,0:T(8,128)(2,1)S(1)} %collective-permute-done.3), channel_id=1, source_target_pairs={{764,0},{0,4},{4,8},{8,12},{12,16},{16,20},{20,24},{24,28},{28,32}... | collective-permute-start | bytes 884744 | tf_op jit(solution)/shard_map/ppermute | solution.py:12
  82.1 10.3 %collective-permute-start.5 = (bf16[128,1152]{1,0:T(8,128)(2,1)S(1)}, bf16[128,1152]{1,0:T(8,128)(2,1)S(1)}, u32[]{:S(2)}, u32[]{:S(2)}) collective-permute-start(bf16[128,1152]{1,0:T(8,128)(2,1)S(1)} %collective-permute-done.4), channel_id=1, source_target_pairs={{764,0},{0,4},{4,8},{8,12},{12,16},{16,20},{20,24},{24,28},{28,32}... | collective-permute-start | bytes 884744 | tf_op jit(solution)/shard_map/ppermute | solution.py:12
  85.9 1.3 copy-start
  95.3 21.1 %collective-permute-start.10 = (f32[128,1152]{1,0:T(8,128)S(1)}, f32[128,1152]{1,0:T(8,128)S(1)}, u32[]{:S(2)}, u32[]{:S(2)}) collective-permute-start(f32[128,1152]{1,0:T(8,128)S(1)} %fusion.63), channel_id=1, source_target_pairs={{8,0},{12,4},{16,8},{20,12},{24,16},{28,20},{32,24},{36,28},{40,32... | collective-permute-start | bytes 1769480 | tf_op jit(solution)/shard_map/ppermute | solution.py:12
  97.6 29.2 %collective-permute-start.9 = (f32[128,1152]{1,0:T(8,128)S(1)}, f32[128,1152]{1,0:T(8,128)S(1)}, u32[]{:S(2)}, u32[]{:S(2)}) collective-permute-start(f32[128,1152]{1,0:T(8,128)S(1)} %fusion.62), channel_id=1, source_target_pairs={{4,0},{8,4},{12,8},{16,12},{20,16},{24,20},{28,24},{32,28},{36,32}... | collective-permute-start | bytes 1769480 | tf_op jit(solution)/shard_map/ppermute | solution.py:12
  103.5 23.3 %collective-permute-start.8 = (f32[128,1152]{1,0:T(8,128)S(1)}, f32[128,1152]{1,0:T(8,128)S(1)}, u32[]{:S(2)}, u32[]{:S(2)}) collective-permute-start(f32[128,1152]{1,0:T(8,128)S(1)} %fusion.61), channel_id=1, source_target_pairs={{764,0},{0,4},{4,8},{8,12},{12,16},{16,20},{20,24},{24,28},{28,32}... | collective-permute-start | bytes 1769480 | tf_op jit(solution)/shard_map/ppermute | solution.py:12
  105.8 32.7 %collective-permute-start.6 = (f32[128,1152]{1,0:T(8,128)S(1)}, f32[128,1152]{1,0:T(8,128)S(1)}, u32[]{:S(2)}, u32[]{:S(2)}) collective-permute-start(f32[128,1152]{1,0:T(8,128)S(1)} %fusion.59), channel_id=1, source_target_pairs={{756,0},{760,4},{764,8},{0,12},{4,16},{8,20},{12,24},{16,28},{20,3... | collective-permute-start | bytes 1769480 | tf_op jit(solution)/shard_map/ppermute | solution.py:12
  109.9 43.0 %collective-permute-start.7 = (f32[128,1152]{1,0:T(8,128)S(1)}, f32[128,1152]{1,0:T(8,128)S(1)}, u32[]{:S(2)}, u32[]{:S(2)}) collective-permute-start(f32[128,1152]{1,0:T(8,128)S(1)} %fusion.60), channel_id=1, source_target_pairs={{760,0},{764,4},{0,8},{4,12},{8,16},{12,20},{16,24},{20,28},{24,32... | collective-permute-start | bytes 1769480 | tf_op jit(solution)/shard_map/ppermute | solution.py:12
  153.4 45.2 %copy-start.2 = (bf16[128,1152]{1,0:T(8,128)(2,1)S(1)}, bf16[128,1152]{1,0:T(8,128)(2,1)}, u32[]{:S(2)}) copy-start(bf16[128,1152]{1,0:T(8,128)(2,1)} %param.5) | copy-start | bytes 884740
  198.7 1.4 copy-start.3
Sparse Core Ops, SparseCore 0:
  11.0 49.4 all-gather.2
  95.0 103.6 reduce-scatter.1
where the time goes:
time: 208 us
  waiting for transfers between devices  117 us (56%)
  starting transfers between devices  45.5 us (22%)
  between operations  15.7 us (8%)
  blocking collectives  10.9 us (5%)
  matrix products  10.9 us (5%)
  other arithmetic  6.67 us (3%)
    ppermute x11, waiting for transfers between devices, shifted(): return lax.ppermute(block, axis, route)  73.2 us
    ppermute x11, starting transfers between devices, shifted(): return lax.ppermute(block, axis, route)  45.4 us
    reduce_scatter x1, waiting for transfers between devices, local(): lax.psum_scatter(image_total_sum, 'rows', scatter_dimension=0, tiled=True)  44.2 us
    all_gather x1, blocking collectives, local(): lax.all_gather(positive_offset, 'rows', axis=0, tiled=True)  10.9 us
    dot_general x6, matrix products, contribute(): lax.dot_general(group_image, paired_side, (((1,), (1,)), ((), ())), prefe...  4.44 us
  transfers between devices with their start and end apart: 13, of which 9 were waited for; matrix products, arithmetic and copies ran while one was open for 5% of the time, Pallas kernels for 0%

commit v1 on v0

v1 whole, which is shorter than its diff:
```python
import jax
import jax.numpy as jnp
from jax import lax
from jax.sharding import PartitionSpec as P


def from_group(block, distance):
    count = lax.axis_size("dp")
    return lax.ppermute(block, "dp", [((i + distance) % count, i) for i in range(count)])


def from_member(block, flip):
    return lax.ppermute(block, "rows", [(i ^ flip, i) for i in range(lax.axis_size("rows"))])


def unit_rows(values):
    widened = values.astype(jnp.float32)
    row_norm = jnp.sqrt(jnp.sum(widened * widened, axis=1, keepdims=True) + 1e-06)
    return widened / row_norm, row_norm


def low_rows(values):
    return unit_rows(values)[0].astype(jnp.bfloat16)


def project_tangent(unit_values, row_norm, direction):
    inner = jnp.sum(unit_values * direction, axis=1, keepdims=True)
    return (direction - unit_values * inner) / row_norm


def local(images, texts, positive_offset, logit_log_scale, bias):
    low = jnp.bfloat16
    quarter = texts.shape[0]
    scale = jnp.exp(logit_log_scale[0])
    target = positive_offset - 2

    images_far = from_member(images, 2)
    texts_at = {0: texts}
    texts_at[1] = from_group(texts, 1)
    texts_at[-1] = from_group(texts, -1)
    texts_at[3] = from_group(texts, 3)
    images_near = from_member(images, 1)
    images_far_near = from_member(images_far, 1)
    texts_at[2] = from_group(texts_at[1], 1)
    texts_at[-2] = from_group(texts_at[-1], -1)

    group = low_rows(jnp.concatenate([images, images_near, images_far, images_far_near]))
    diagonal = jnp.arange(group.shape[0])[:, None] == jnp.arange(quarter)[None, :]

    image_sum = jnp.zeros(group.shape, jnp.float32)
    text_part = {}
    for offset in (0, 1, -1, 3, 2, -2):
        text = low_rows(texts_at[offset])
        scores = lax.dot_general(
            group, text, (((1,), (1,)), ((), ())), preferred_element_type=jnp.float32
        )
        logits = scale * scores + bias[0]
        positive = jnp.logical_and((target == offset)[None, :], diagonal)
        sign = jnp.where(positive, 1.0, -1.0).astype(jnp.float32)
        weights = (-sign * jax.nn.sigmoid(-sign * logits)).astype(low)
        image_sum = image_sum + jnp.dot(weights, text, preferred_element_type=jnp.float32)
        text_part[offset] = lax.dot_general(
            weights, group, (((0,), (0,)), ((), ())), preferred_element_type=jnp.float32
        )

    def home(part, distance):
        return from_group(part.astype(low), -distance).astype(jnp.float32)

    above = text_part[1] + home(text_part[2], 1)
    below = text_part[-1] + home(text_part[-2], -1)
    text_total = text_part[0] + home(text_part[3], 3) + home(above, 1) + home(below, -1)

    parts = image_sum.reshape(4, quarter, -1)
    near = from_member(parts[1::2].astype(low), 1).astype(jnp.float32)
    parts = parts[0::2] + near
    image_total = parts[0] + from_member(parts[1].astype(low), 2).astype(jnp.float32)

    image_gradient = project_tangent(*unit_rows(images), scale * image_total)
    text_gradient = project_tangent(*unit_rows(texts), scale * text_total)
    return image_gradient, text_gradient


def solution(mesh):
    return jax.shard_map(
        local,
        mesh=mesh,
        in_specs=(P(("dp", "rows"), None), P(("dp", "rows"), None), P(("dp", "rows")), P(), P()),
        out_specs=(P(("dp", "rows"), None), P(("dp", "rows"), None)),
        check_vma=False,
    )
```

time: 208 us -> 109 us (0.52)
  the two profiles are of different devices: /device:TPU:15 before, /device:TPU:1 now
where the time goes in v1:
time: 109 us
  starting transfers between devices  75.6 us (69%)
  waiting for transfers between devices  14.2 us (13%)
  matrix products  9.31 us (9%)
  other arithmetic  6.94 us (6%)
  between operations  2.37 us (2%)
    ppermute x10, starting transfers between devices, from_group(): lax.ppermute(block, 'dp', [((i + distance) % count, i) for i in range(cou...  48.5 us
    ppermute x5, starting transfers between devices, from_member(): lax.ppermute(block, 'rows', [(i ^ flip, i) for i in range(lax.axis_size('...  27 us
    ppermute x10, waiting for transfers between devices, from_group(): lax.ppermute(block, 'dp', [((i + distance) % count, i) for i in range(cou...  11.9 us
    dot_general x6, matrix products, local(): lax.dot_general(group, text, (((1,), (1,)), ((), ())), preferred_element_...  3.56 us
    dot_general x6, matrix products, local(): jnp.dot(weights, text, preferred_element_type=jnp.float32)  3.3 us
    reduce_sum x8, other arithmetic, unit_rows(): jnp.sum(widened * widened, axis=1, keepdims=True) + 1e-06  3.22 us
    dot_general x6, matrix products, local(): lax.dot_general(weights, group, (((0,), (0,)), ((), ())), preferred_eleme...  2.46 us
    ppermute x5, waiting for transfers between devices, from_member(): lax.ppermute(block, 'rows', [(i ^ flip, i) for i in range(lax.axis_size('...  2.35 us
  transfers between devices with their start and end apart: 15, of which 4 were waited for; matrix products, arithmetic and copies ran while one was open for 14% of the time, Pallas kernels for 0%

profile of v1, /device:TPU:1, one launch (start us, length us, event | category | flops | bytes accessed | tf_op | source)
XLA Modules:
  0.0 108.5 jit_solution(3044230860550949869)
XLA Ops:
  0.6 0.0 copy-start
  0.6 8.4 %collective-permute-start.1 = (bf16[128,1152]{1,0:T(8,128)(2,1)}, bf16[128,1152]{1,0:T(8,128)(2,1)S(1)}, u32[]{:S(2)}, u32[]{:S(2)}) collective-permute-start(bf16[128,1152]{1,0:T(8,128)(2,1)} %param.5), channel_id=1, source_target_pairs={{2,0},{3,1},{0,2},{1,3},{6,4},{7,5},{4,6},{5,7},{10,8},{11,9},{8,1... | collective-permute-start | bytes 884744 | tf_op jit(solution)/shard_map/ppermute | solution.py:13
  9.1 6.1 %collective-permute-start = (bf16[128,1152]{1,0:T(8,128)(2,1)}, bf16[128,1152]{1,0:T(8,128)(2,1)S(1)}, u32[]{:S(2)}, u32[]{:S(2)}) collective-permute-start(bf16[128,1152]{1,0:T(8,128)(2,1)} %param.5), channel_id=1, source_target_pairs={{1,0},{0,1},{3,2},{2,3},{5,4},{4,5},{7,6},{6,7},{9,8},{8,9},{11,10... | collective-permute-start | bytes 884744 | tf_op jit(solution)/shard_map/ppermute | solution.py:13
  15.1 13.6 %collective-permute-start.3 = (bf16[128,1152]{1,0:T(8,128)(2,1)}, bf16[128,1152]{1,0:T(8,128)(2,1)S(1)}, u32[]{:S(2)}, u32[]{:S(2)}) collective-permute-start(bf16[128,1152]{1,0:T(8,128)(2,1)} %param.6), channel_id=1, source_target_pairs={{4,0},{8,4},{12,8},{16,12},{20,16},{24,20},{28,24},{32,28},{36,32}... | collective-permute-start | bytes 884744 | tf_op jit(solution)/shard_map/ppermute | solution.py:9
  28.8 1.9 %collective-permute-start.4 = (bf16[128,1152]{1,0:T(8,128)(2,1)}, bf16[128,1152]{1,0:T(8,128)(2,1)S(1)}, u32[]{:S(2)}, u32[]{:S(2)}) collective-permute-start(bf16[128,1152]{1,0:T(8,128)(2,1)} %param.6), channel_id=1, source_target_pairs={{764,0},{0,4},{4,8},{8,12},{12,16},{16,20},{20,24},{24,28},{28,32}... | collective-permute-start | bytes 884744 | tf_op jit(solution)/shard_map/ppermute | solution.py:9
  30.7 2.1 %collective-permute-start.5 = (bf16[128,1152]{1,0:T(8,128)(2,1)}, bf16[128,1152]{1,0:T(8,128)(2,1)S(1)}, u32[]{:S(2)}, u32[]{:S(2)}) collective-permute-start(bf16[128,1152]{1,0:T(8,128)(2,1)} %param.6), channel_id=1, source_target_pairs={{12,0},{16,4},{20,8},{24,12},{28,16},{32,20},{36,24},{40,28},{44,3... | collective-permute-start | bytes 884744 | tf_op jit(solution)/shard_map/ppermute | solution.py:9
  32.8 1.1 %fusion.52 = f32[128]{0:T(128)S(1)} fusion(bf16[128,1152]{1,0:T(8,128)(2,1)} %param.6), kind=kLoop, calls=%fused_computation.82 | loop fusion | flops 442240 | bytes 295424 | tf_op jit(solution)/shard_map/reduce_sum | solution.py:18
  33.9 1.1 %fusion.63 = f32[128]{0:T(128)S(1)} fusion(bf16[128,1152]{1,0:T(8,128)(2,1)} %param.5), kind=kLoop, calls=%fused_computation.93 | loop fusion | flops 442240 | bytes 295424 | tf_op jit(solution)/shard_map/reduce_sum | solution.py:18
  36.4 0.7 broadcast_compare_fusion
  37.1 0.0 collective-permute-done.1
  37.1 4.4 %collective-permute-start.2 = (bf16[128,1152]{1,0:T(8,128)(2,1)S(1)}, bf16[128,1152]{1,0:T(8,128)(2,1)S(1)}, u32[]{:S(2)}, u32[]{:S(2)}) collective-permute-start(bf16[128,1152]{1,0:T(8,128)(2,1)S(1)} %collective-permute-done.1), channel_id=1, source_target_pairs={{1,0},{0,1},{3,2},{2,3},{5,4},{4,5},{7,6},{6,7},{9,8},{8,9},{11,10... | collective-permute-start | bytes 884744 | tf_op jit(solution)/shard_map/ppermute | solution.py:13
  41.4 0.0 collective-permute-done.3
  41.5 7.3 %collective-permute-start.6 = (bf16[128,1152]{1,0:T(8,128)(2,1)S(1)}, bf16[128,1152]{1,0:T(8,128)(2,1)S(1)}, u32[]{:S(2)}, u32[]{:S(2)}) collective-permute-start(bf16[128,1152]{1,0:T(8,128)(2,1)S(1)} %collective-permute-done.3), channel_id=1, source_target_pairs={{4,0},{8,4},{12,8},{16,12},{20,16},{24,20},{28,24},{32,28},{36,32}... | collective-permute-start | bytes 884744 | tf_op jit(solution)/shard_map/ppermute | solution.py:9
  48.8 0.1 fusion.53
  48.9 0.0 collective-permute-done.4
  48.9 1.9 %collective-permute-start.7 = (bf16[128,1152]{1,0:T(8,128)(2,1)S(1)}, bf16[128,1152]{1,0:T(8,128)(2,1)S(1)}, u32[]{:S(2)}, u32[]{:S(2)}) collective-permute-start(bf16[128,1152]{1,0:T(8,128)(2,1)S(1)} %collective-permute-done.4), channel_id=1, source_target_pairs={{764,0},{0,4},{4,8},{8,12},{12,16},{16,20},{20,24},{24,28},{28,32}... | collective-permute-start | bytes 884744 | tf_op jit(solution)/shard_map/ppermute | solution.py:9
  50.9 0.1 fusion.55
  51.0 0.0 collective-permute-done.5
  51.0 0.1 fusion.57
  51.2 0.0 collective-permute-done
  51.2 0.0 collective-permute-done.2
  51.2 0.3 fusion.2
  51.5 2.8 %collective-permute-done.6 = bf16[128,1152]{1,0:T(8,128)(2,1)S(1)} collective-permute-done((bf16[128,1152]{1,0:T(8,128)(2,1)S(1)}, bf16[128,1152]{1,0:T(8,128)(2,1)S(1)}, u32[]{:S(2)}, u32[]{:S(2)}) %collective-permute-start.6) | collective-permute-done | bytes 294944 | tf_op jit(solution)/shard_map/ppermute | solution.py:9
  54.4 0.1 fusion.59
  54.5 0.4 fusion.3
  54.9 0.6 fusion.47
  55.5 0.4 convolution_convert_fusion.1
  55.9 4.8 %collective-permute-start.11 = (bf16[128,1152]{1,0:T(8,128)(2,1)S(1)}, bf16[128,1152]{1,0:T(8,128)(2,1)S(1)}, u32[]{:S(2)}, u32[]{:S(2)}) collective-permute-start(bf16[128,1152]{1,0:T(8,128)(2,1)S(1)} %convolution_convert_fusion.1), channel_id=1, source_target_pairs={{764,0},{0,4},{4,8},{8,12},{12,16},{16,20},{20,24},{24,28},{28,32}... | collective-permute-start | bytes 884744 | tf_op jit(solution)/shard_map/ppermute | solution.py:9
  60.7 3.6 %collective-permute-done.7 = bf16[128,1152]{1,0:T(8,128)(2,1)S(1)} collective-permute-done((bf16[128,1152]{1,0:T(8,128)(2,1)S(1)}, bf16[128,1152]{1,0:T(8,128)(2,1)S(1)}, u32[]{:S(2)}, u32[]{:S(2)}) %collective-permute-start.7) | collective-permute-done | bytes 294944 | tf_op jit(solution)/shard_map/ppermute | solution.py:9
  64.4 0.1 fusion.61
  64.5 0.6 fusion.46
  65.1 0.0 copy-start.1
  65.1 0.4 convolution_convert_fusion
  65.5 3.6 %collective-permute-start.13 = (bf16[128,1152]{1,0:T(8,128)(2,1)S(1)}, bf16[128,1152]{1,0:T(8,128)(2,1)S(1)}, u32[]{:S(2)}, u32[]{:S(2)}) collective-permute-start(bf16[128,1152]{1,0:T(8,128)(2,1)S(1)} %convolution_convert_fusion), channel_id=1, source_target_pairs={{4,0},{8,4},{12,8},{16,12},{20,16},{24,20},{28,24},{32,28},{36,32}... | collective-permute-start | bytes 884744 | tf_op jit(solution)/shard_map/ppermute | solution.py:9
  69.1 0.6 fusion.51
  69.7 0.5 fusion.73
  70.3 0.5 fusion.76
  70.8 0.6 fusion.48
  71.4 0.5 fusion.81
  72.0 0.6 fusion.50
  72.6 0.5 convolution_add_fusion.2
  73.1 0.6 fusion.49
  73.7 0.5 fusion
  74.2 0.6 fusion.1
  74.9 0.1 convert.6
  75.0 3.8 %collective-permute-start.8 = (bf16[2,128,1152]{2,1,0:T(8,128)(2,1)S(1)}, bf16[2,128,1152]{2,1,0:T(8,128)(2,1)S(1)}, u32[]{:S(2)}, u32[]{:S(2)}) collective-permute-start(bf16[2,128,1152]{2,1,0:T(8,128)(2,1)S(1)} %slice.15), channel_id=1, source_target_pairs={{1,0},{0,1},{3,2},{2,3},{5,4},{4,5},{7,6},{6,7},{9,8},{8,9},{11,10... | collective-permute-start | bytes 1769480 | tf_op jit(solution)/shard_map/ppermute | solution.py:13
  78.8 0.4 convolution_convert_fusion.2
  79.2 1.9 %collective-permute-start.10 = (bf16[128,1152]{1,0:T(8,128)(2,1)S(1)}, bf16[128,1152]{1,0:T(8,128)(2,1)S(1)}, u32[]{:S(2)}, u32[]{:S(2)}) collective-permute-start(bf16[128,1152]{1,0:T(8,128)(2,1)S(1)} %convolution_convert_fusion.2), channel_id=1, source_target_pairs={{756,0},{760,4},{764,8},{0,12},{4,16},{8,20},{12,24},{16,28},{20,3... | collective-permute-start | bytes 884744 | tf_op jit(solution)/shard_map/ppermute | solution.py:9
  81.2 0.0 collective-permute-done.11
  81.2 0.4 add_convert_fusion.1
  81.6 2.0 %collective-permute-start.12 = (bf16[128,1152]{1,0:T(8,128)(2,1)S(1)}, bf16[128,1152]{1,0:T(8,128)(2,1)S(1)}, u32[]{:S(2)}, u32[]{:S(2)}) collective-permute-start(bf16[128,1152]{1,0:T(8,128)(2,1)S(1)} %add_convert_fusion.1), channel_id=1, source_target_pairs={{764,0},{0,4},{4,8},{8,12},{12,16},{16,20},{20,24},{24,28},{28,32}... | collective-permute-start | bytes 884744 | tf_op jit(solution)/shard_map/ppermute | solution.py:9
  83.5 0.0 collective-permute-done.13
  83.6 0.4 add_convert_fusion
  83.9 9.3 %collective-permute-start.14 = (bf16[128,1152]{1,0:T(8,128)(2,1)S(1)}, bf16[128,1152]{1,0:T(8,128)(2,1)S(1)}, u32[]{:S(2)}, u32[]{:S(2)}) collective-permute-start(bf16[128,1152]{1,0:T(8,128)(2,1)S(1)} %add_convert_fusion), channel_id=1, source_target_pairs={{4,0},{8,4},{12,8},{16,12},{20,16},{24,20},{28,24},{32,28},{36,32}... | collective-permute-start | bytes 884744 | tf_op jit(solution)/shard_map/ppermute | solution.py:9
  93.3 0.0 collective-permute-done.8
  93.3 0.1 convert_add_fusion
  93.4 4.4 %collective-permute-start.9 = (bf16[128,1152]{1,0:T(8,128)(2,1)S(1)}, bf16[128,1152]{1,0:T(8,128)(2,1)S(1)}, u32[]{:S(2)}, u32[]{:S(2)}) collective-permute-start(bf16[128,1152]{1,0:T(8,128)(2,1)S(1)} %fusion.66), channel_id=1, source_target_pairs={{2,0},{3,1},{0,2},{1,3},{6,4},{7,5},{4,6},{5,7},{10,8},{11,9},{8,1... | collective-permute-start | bytes 884744 | tf_op jit(solution)/shard_map/ppermute | solution.py:13
  97.8 0.0 collective-permute-done.10
  97.9 5.4 %collective-permute-done.12 = bf16[128,1152]{1,0:T(8,128)(2,1)S(1)} collective-permute-done((bf16[128,1152]{1,0:T(8,128)(2,1)S(1)}, bf16[128,1152]{1,0:T(8,128)(2,1)S(1)}, u32[]{:S(2)}, u32[]{:S(2)}) %collective-permute-start.12) | collective-permute-done | bytes 294944 | tf_op jit(solution)/shard_map/ppermute | solution.py:9
  103.2 0.6 multiply_reduce_fusion
  103.8 1.1 %subtract_divide_fusion = f32[128,1152]{1,0:T(8,128)} fusion(f32[128]{0:T(128)S(1)} %get-tuple-element.8, f32[128]{0:T(128)S(1)} %add_sqrt_fusion.7, bf16[128,1152]{1,0:T(8,128)(2,1)S(1)} %collective-permute-done.14, bf16[128,1152]{1,0:T(8,128)(2,1)S(1)} %collective-permute-done.12, f32[128,1152]{1,0:T(8,128)S(1)} %get-tuple-element.9, ...), kind=kLoop, calls=%fused_computation.98 | loop fusion | flops 1769472 | bytes 2360324 | tf_op jit(solution)/shard_map/div | solution.py:28
  104.9 2.3 %collective-permute-done.9 = bf16[128,1152]{1,0:T(8,128)(2,1)S(1)} collective-permute-done((bf16[128,1152]{1,0:T(8,128)(2,1)S(1)}, bf16[128,1152]{1,0:T(8,128)(2,1)S(1)}, u32[]{:S(2)}, u32[]{:S(2)}) %collective-permute-start.9) | collective-permute-done | bytes 294944 | tf_op jit(solution)/shard_map/ppermute | solution.py:13
  107.2 0.3 multiply_reduce_fusion.1
  107.5 1.0 subtract_divide_fusion.1
  (13 shorter events, 0.2 us)
Async XLA Ops:
  0.6 50.6 %copy-start = (bf16[128,1152]{1,0:T(8,128)(2,1)S(1)}, bf16[128,1152]{1,0:T(8,128)(2,1)}, u32[]{:S(2)}) copy-start(bf16[128,1152]{1,0:T(8,128)(2,1)} %param.5) | copy-start | bytes 884740
  0.6 36.4 %collective-permute-start.1 = (bf16[128,1152]{1,0:T(8,128)(2,1)}, bf16[128,1152]{1,0:T(8,128)(2,1)S(1)}, u32[]{:S(2)}, u32[]{:S(2)}) collective-permute-start(bf16[128,1152]{1,0:T(8,128)(2,1)} %param.5), channel_id=1, source_target_pairs={{2,0},{3,1},{0,2},{1,3},{6,4},{7,5},{4,6},{5,7},{10,8},{11,9},{8,1... | collective-permute-start | bytes 884744 | tf_op jit(solution)/shard_map/ppermute | solution.py:13
  9.1 42.1 %collective-permute-start = (bf16[128,1152]{1,0:T(8,128)(2,1)}, bf16[128,1152]{1,0:T(8,128)(2,1)S(1)}, u32[]{:S(2)}, u32[]{:S(2)}) collective-permute-start(bf16[128,1152]{1,0:T(8,128)(2,1)} %param.5), channel_id=1, source_target_pairs={{1,0},{0,1},{3,2},{2,3},{5,4},{4,5},{7,6},{6,7},{9,8},{8,9},{11,10... | collective-permute-start | bytes 884744 | tf_op jit(solution)/shard_map/ppermute | solution.py:13
  15.1 26.3 %collective-permute-start.3 = (bf16[128,1152]{1,0:T(8,128)(2,1)}, bf16[128,1152]{1,0:T(8,128)(2,1)S(1)}, u32[]{:S(2)}, u32[]{:S(2)}) collective-permute-start(bf16[128,1152]{1,0:T(8,128)(2,1)} %param.6), channel_id=1, source_target_pairs={{4,0},{8,4},{12,8},{16,12},{20,16},{24,20},{28,24},{32,28},{36,32}... | collective-permute-start | bytes 884744 | tf_op jit(solution)/shard_map/ppermute | solution.py:9
  28.8 20.2 %collective-permute-start.4 = (bf16[128,1152]{1,0:T(8,128)(2,1)}, bf16[128,1152]{1,0:T(8,128)(2,1)S(1)}, u32[]{:S(2)}, u32[]{:S(2)}) collective-permute-start(bf16[128,1152]{1,0:T(8,128)(2,1)} %param.6), channel_id=1, source_target_pairs={{764,0},{0,4},{4,8},{8,12},{12,16},{16,20},{20,24},{24,28},{28,32}... | collective-permute-start | bytes 884744 | tf_op jit(solution)/shard_map/ppermute | solution.py:9
  30.7 20.3 %collective-permute-start.5 = (bf16[128,1152]{1,0:T(8,128)(2,1)}, bf16[128,1152]{1,0:T(8,128)(2,1)S(1)}, u32[]{:S(2)}, u32[]{:S(2)}) collective-permute-start(bf16[128,1152]{1,0:T(8,128)(2,1)} %param.6), channel_id=1, source_target_pairs={{12,0},{16,4},{20,8},{24,12},{28,16},{32,20},{36,24},{40,28},{44,3... | collective-permute-start | bytes 884744 | tf_op jit(solution)/shard_map/ppermute | solution.py:9
  37.1 14.1 %collective-permute-start.2 = (bf16[128,1152]{1,0:T(8,128)(2,1)S(1)}, bf16[128,1152]{1,0:T(8,128)(2,1)S(1)}, u32[]{:S(2)}, u32[]{:S(2)}) collective-permute-start(bf16[128,1152]{1,0:T(8,128)(2,1)S(1)} %collective-permute-done.1), channel_id=1, source_target_pairs={{1,0},{0,1},{3,2},{2,3},{5,4},{4,5},{7,6},{6,7},{9,8},{8,9},{11,10... | collective-permute-start | bytes 884744 | tf_op jit(solution)/shard_map/ppermute | solution.py:13
  41.5 12.9 %collective-permute-start.6 = (bf16[128,1152]{1,0:T(8,128)(2,1)S(1)}, bf16[128,1152]{1,0:T(8,128)(2,1)S(1)}, u32[]{:S(2)}, u32[]{:S(2)}) collective-permute-start(bf16[128,1152]{1,0:T(8,128)(2,1)S(1)} %collective-permute-done.3), channel_id=1, source_target_pairs={{4,0},{8,4},{12,8},{16,12},{20,16},{24,20},{28,24},{32,28},{36,32}... | collective-permute-start | bytes 884744 | tf_op jit(solution)/shard_map/ppermute | solution.py:9
  48.9 15.4 %collective-permute-start.7 = (bf16[128,1152]{1,0:T(8,128)(2,1)S(1)}, bf16[128,1152]{1,0:T(8,128)(2,1)S(1)}, u32[]{:S(2)}, u32[]{:S(2)}) collective-permute-start(bf16[128,1152]{1,0:T(8,128)(2,1)S(1)} %collective-permute-done.4), channel_id=1, source_target_pairs={{764,0},{0,4},{4,8},{8,12},{12,16},{16,20},{20,24},{24,28},{28,32}... | collective-permute-start | bytes 884744 | tf_op jit(solution)/shard_map/ppermute | solution.py:9
  55.9 25.3 %collective-permute-start.11 = (bf16[128,1152]{1,0:T(8,128)(2,1)S(1)}, bf16[128,1152]{1,0:T(8,128)(2,1)S(1)}, u32[]{:S(2)}, u32[]{:S(2)}) collective-permute-start(bf16[128,1152]{1,0:T(8,128)(2,1)S(1)} %convolution_convert_fusion.1), channel_id=1, source_target_pairs={{764,0},{0,4},{4,8},{8,12},{12,16},{16,20},{20,24},{24,28},{28,32}... | collective-permute-start | bytes 884744 | tf_op jit(solution)/shard_map/ppermute | solution.py:9
  65.1 4.0 %copy-start.1 = (bf16[128,1152]{1,0:T(8,128)(2,1)S(1)}, bf16[128,1152]{1,0:T(8,128)(2,1)}, u32[]{:S(2)}) copy-start(bf16[128,1152]{1,0:T(8,128)(2,1)} %param.6) | copy-start | bytes 884740
  65.5 18.0 %collective-permute-start.13 = (bf16[128,1152]{1,0:T(8,128)(2,1)S(1)}, bf16[128,1152]{1,0:T(8,128)(2,1)S(1)}, u32[]{:S(2)}, u32[]{:S(2)}) collective-permute-start(bf16[128,1152]{1,0:T(8,128)(2,1)S(1)} %convolution_convert_fusion), channel_id=1, source_target_pairs={{4,0},{8,4},{12,8},{16,12},{20,16},{24,20},{28,24},{32,28},{36,32}... | collective-permute-start | bytes 884744 | tf_op jit(solution)/shard_map/ppermute | solution.py:9
  75.0 18.2 %collective-permute-start.8 = (bf16[2,128,1152]{2,1,0:T(8,128)(2,1)S(1)}, bf16[2,128,1152]{2,1,0:T(8,128)(2,1)S(1)}, u32[]{:S(2)}, u32[]{:S(2)}) collective-permute-start(bf16[2,128,1152]{2,1,0:T(8,128)(2,1)S(1)} %slice.15), channel_id=1, source_target_pairs={{1,0},{0,1},{3,2},{2,3},{5,4},{4,5},{7,6},{6,7},{9,8},{8,9},{11,10... | collective-permute-start | bytes 1769480 | tf_op jit(solution)/shard_map/ppermute | solution.py:13
  79.2 18.6 %collective-permute-start.10 = (bf16[128,1152]{1,0:T(8,128)(2,1)S(1)}, bf16[128,1152]{1,0:T(8,128)(2,1)S(1)}, u32[]{:S(2)}, u32[]{:S(2)}) collective-permute-start(bf16[128,1152]{1,0:T(8,128)(2,1)S(1)} %convolution_convert_fusion.2), channel_id=1, source_target_pairs={{756,0},{760,4},{764,8},{0,12},{4,16},{8,20},{12,24},{16,28},{20,3... | collective-permute-start | bytes 884744 | tf_op jit(solution)/shard_map/ppermute | solution.py:9
  81.6 21.7 %collective-permute-start.12 = (bf16[128,1152]{1,0:T(8,128)(2,1)S(1)}, bf16[128,1152]{1,0:T(8,128)(2,1)S(1)}, u32[]{:S(2)}, u32[]{:S(2)}) collective-permute-start(bf16[128,1152]{1,0:T(8,128)(2,1)S(1)} %add_convert_fusion.1), channel_id=1, source_target_pairs={{764,0},{0,4},{4,8},{8,12},{12,16},{16,20},{20,24},{24,28},{28,32}... | collective-permute-start | bytes 884744 | tf_op jit(solution)/shard_map/ppermute | solution.py:9
  83.9 19.3 %collective-permute-start.14 = (bf16[128,1152]{1,0:T(8,128)(2,1)S(1)}, bf16[128,1152]{1,0:T(8,128)(2,1)S(1)}, u32[]{:S(2)}, u32[]{:S(2)}) collective-permute-start(bf16[128,1152]{1,0:T(8,128)(2,1)S(1)} %add_convert_fusion), channel_id=1, source_target_pairs={{4,0},{8,4},{12,8},{16,12},{20,16},{24,20},{28,24},{32,28},{36,32}... | collective-permute-start | bytes 884744 | tf_op jit(solution)/shard_map/ppermute | solution.py:9
  93.4 13.8 %collective-permute-start.9 = (bf16[128,1152]{1,0:T(8,128)(2,1)S(1)}, bf16[128,1152]{1,0:T(8,128)(2,1)S(1)}, u32[]{:S(2)}, u32[]{:S(2)}) collective-permute-start(bf16[128,1152]{1,0:T(8,128)(2,1)S(1)} %fusion.66), channel_id=1, source_target_pairs={{2,0},{3,1},{0,2},{1,3},{6,4},{7,5},{4,6},{5,7},{10,8},{11,9},{8,1... | collective-permute-start | bytes 884744 | tf_op jit(solution)/shard_map/ppermute | solution.py:13

commit v2 on v1

v2 whole, which is shorter than its diff:
```python
import jax
import jax.numpy as jnp
from jax import lax
from jax.experimental import pallas as pl
from jax.experimental.pallas import tpu as pltpu
from jax.sharding import PartitionSpec as P

MEMBERS = 4
VMEM = pl.BlockSpec(memory_space=pltpu.VMEM)
SMEM = pl.BlockSpec(memory_space=pltpu.SMEM)
LIMIT = 32 << 20
LOW, WIDE = jnp.bfloat16, jnp.float32


def from_member(block, flip):
    return lax.ppermute(block, "rows", [(i ^ flip, i) for i in range(MEMBERS)])


def from_group(block, distance):
    count = lax.axis_size("dp")
    return lax.ppermute(block, "dp", [((i + distance) % count, i) for i in range(count)])


def kernel_call(body, outs, *args):
    return pl.pallas_call(
        body,
        out_shape=[jax.ShapeDtypeStruct(s, d) for s, d in outs],
        in_specs=[SMEM if a.ndim == 1 else VMEM for a in args],
        out_specs=[VMEM] * len(outs),
        compiler_params=pltpu.CompilerParams(vmem_limit_bytes=LIMIT),
        cost_estimate=pl.CostEstimate(flops=0, bytes_accessed=0, transcendentals=0),
    )(*args)


def unit_rows(raw):
    wide = raw.astype(WIDE)
    inverse = lax.rsqrt(jnp.sum(wide * wide, axis=1, keepdims=True) + 1e-06)
    return wide * inverse, inverse


def tangent(unit, direction):
    return direction - unit * jnp.sum(unit * direction, axis=1, keepdims=True)


def sigmoid(values):
    return 1.0 / (1.0 + jnp.exp(-values))


def meet(group, text, scalars, target, offsets):
    quarter = target.shape[1]
    scores = lax.dot_general(
        group, text, (((1,), (1,)), ((), ())), preferred_element_type=WIDE
    )
    logits = scalars[0] * scores + scalars[1]
    row = lax.broadcasted_iota(jnp.int32, (quarter, quarter), 0)
    diagonal = row == lax.broadcasted_iota(jnp.int32, (quarter, quarter), 1)
    own = []
    for i, offset in enumerate(offsets):
        block = logits[:quarter, i * quarter : (i + 1) * quarter]
        sign = jnp.where(jnp.logical_and(diagonal, target == offset), -1.0, 1.0)
        own.append(sign * sigmoid(sign * block))
    own = jnp.concatenate(own, axis=1).astype(LOW)
    weights = jnp.concatenate([own, sigmoid(logits[quarter:]).astype(LOW)])
    image_part = jnp.dot(weights, text, preferred_element_type=WIDE)
    text_part = lax.dot_general(
        weights, group, (((0,), (0,)), ((), ())), preferred_element_type=WIDE
    )
    return image_part, text_part


def first_body(
    scalars, a, b, c, d, text, ahead, behind, third, target,
    image_sum, mine, back_1, back_m1, back_3,
):
    quarter = text.shape[0]
    group = jnp.concatenate([unit_rows(s[...])[0].astype(LOW) for s in (a, b, c, d)])
    units = [unit_rows(s[...])[0] for s in (text, ahead, behind, third)]
    low = jnp.concatenate([u.astype(LOW) for u in units])
    image_part, text_part = meet(group, low, scalars, target[...], (0, 1, -1, 3))
    image_sum[...] = image_part
    parts = [tangent(u, text_part[i * quarter : (i + 1) * quarter]) for i, u in enumerate(units)]
    mine[...] = parts[0]
    back_1[...] = parts[1].astype(LOW)
    back_m1[...] = parts[2].astype(LOW)
    back_3[...] = parts[3].astype(LOW)


def second_body(
    scalars, a, b, c, d, ahead, behind, target, so_far, send, kept, back_2, back_m2
):
    quarter = a.shape[0]
    units = [unit_rows(s[...])[0] for s in (a, b, c, d)]
    group = jnp.concatenate([u.astype(LOW) for u in units])
    text_units = [unit_rows(s[...])[0] for s in (ahead, behind)]
    low = jnp.concatenate([u.astype(LOW) for u in text_units])
    image_part, text_part = meet(group, low, scalars, target[...], (2, -2))
    back_2[...] = tangent(text_units[0], text_part[:quarter]).astype(LOW)
    back_m2[...] = tangent(text_units[1], text_part[quarter:]).astype(LOW)
    total = so_far[...] + image_part
    parts = [tangent(u, total[i * quarter : (i + 1) * quarter]) for i, u in enumerate(units)]
    send[0] = parts[1].astype(LOW)
    send[1] = parts[3].astype(LOW)
    kept[0] = parts[0]
    kept[1] = parts[2]


def merge_body(kept, near, own, far):
    own[...] = kept[0] + near[0].astype(WIDE)
    far[...] = (kept[1] + near[1].astype(WIDE)).astype(LOW)


def image_body(scalars, raw, own, far, out):
    _, inverse = unit_rows(raw[...])
    out[...] = (scalars[0] * inverse) * (own[...] + far[...].astype(WIDE))


def text_body(scalars, raw, mine, *parts):
    *parts, out = parts
    _, inverse = unit_rows(raw[...])
    total = mine[...]
    for part in parts:
        total = total + part[...].astype(WIDE)
    out[...] = (scalars[0] * inverse) * total


def local(images, texts, positive_offset, logit_log_scale, bias):
    quarter, width = texts.shape
    shard, two, four = (quarter, width), (2 * quarter, width), (MEMBERS * quarter, width)
    count = lax.axis_size("dp")
    scalars = jnp.concatenate([jnp.exp(logit_log_scale), bias])
    target = (positive_offset - 2).reshape(1, quarter)

    images_far = from_member(images, 2)
    text = {0: texts}
    text[3] = from_group(texts, 3)
    text[-1] = from_group(texts, -1)
    text[1] = from_group(texts, 1)
    images_near = from_member(images, 1)
    images_far_near = from_member(images_far, 1)
    column = lax.axis_index("dp") % 4
    line = [(i // 4 * 4 + (i - 1) % 4, i) for i in range(count)]
    text[2] = lax.ppermute(jnp.where(column == 3, text[-1], text[3]), "dp", line)
    text[-2] = from_group(text[-1], -1)
    group = (images, images_near, images_far, images_far_near)

    image_sum, mine, back_1, back_m1, back_3 = kernel_call(
        first_body,
        [(four, WIDE), (shard, WIDE), (shard, LOW), (shard, LOW), (shard, LOW)],
        scalars, *group, text[0], text[1], text[-1], text[3], target,
    )
    home_3 = from_group(back_3, -3)
    home_1 = from_group(back_1, -1)
    home_m1 = from_group(back_m1, 1)
    send, kept, back_2, back_m2 = kernel_call(
        second_body,
        [((2, *shard), LOW), ((2, *shard), WIDE), (shard, LOW), (shard, LOW)],
        scalars, *group, text[2], text[-2], target, image_sum,
    )
    near = from_member(send, 1)
    home_2 = from_group(back_2, -2)
    home_m2 = from_group(back_m2, 2)
    own, far = kernel_call(merge_body, [(shard, WIDE), (shard, LOW)], kept, near)
    far = from_member(far, 2)
    (text_gradient,) = kernel_call(
        text_body, [(shard, WIDE)], scalars, texts, mine, home_1, home_m1, home_3, home_2, home_m2
    )
    (image_gradient,) = kernel_call(image_body, [(shard, WIDE)], scalars, images, own, far)
    return image_gradient, text_gradient


def solution(mesh):
    return jax.shard_map(
        local,
        mesh=mesh,
        in_specs=(P(("dp", "rows"), None), P(("dp", "rows"), None), P(("dp", "rows")), P(), P()),
        out_specs=(P(("dp", "rows"), None), P(("dp", "rows"), None)),
        check_vma=False,
    )
```

time: 109 us -> 106 us (0.972)
  Pallas kernels: 0 us -> 10.3 us
  matrix products: 9.31 us -> 0 us
  other arithmetic: 6.94 us -> 0.77 us
  local copies, waits for them, and re-layouts: 0.09 us -> 1.93 us
  starting transfers between devices: 75.6 us -> 76.9 us
    pallas_call x0 -> x5, Pallas kernels: none -> 10.3 us  [kernel_call(): pl.pallas_call(body, out_shape=[jax.ShapeDtypeStruct(s, d) for s, d in ou...]
    dot_general x18 -> x0, matrix products: 9.31 us -> none  [the longest x6 3.56 us: local(): lax.dot_general(group, text, (((1,), (1,)), ((), ())), preferred_element_...]
    ppermute x10 -> x9, starting transfers between devices: 48.5 us -> 57.1 us  [from_group(): lax.ppermute(block, 'dp', [((i + distance) % count, i) for i in range(cou...]
    ppermute x5 -> x6, starting transfers between devices: 27 us -> 19.8 us  [the longest x5 17.8 us: from_member(): return lax.ppermute(block, 'rows', [(i ^ flip, i) for i in range(MEMBERS)])]
    reduce_sum x9 -> x0, other arithmetic: 3.47 us -> none  [the longest x8 3.22 us: unit_rows(): jnp.sum(widened * widened, axis=1, keepdims=True) + 1e-06]
    ppermute x5 -> x6, waiting for transfers between devices: 2.35 us -> 0.06 us  [the longest x5 0.06 us: from_member(): return lax.ppermute(block, 'rows', [(i ^ flip, i) for i in range(MEMBERS)])]
    div x2 -> x0, other arithmetic: 2.12 us -> none  [project_tangent(): return (direction - unit_values * inner) / row_norm]
    unnamed x4 -> x8, local copies, waits for them, and re-layouts: 0.01 us -> 1.93 us
  transfers between devices with their start and end apart: 15 -> 15, of which waited for: 4 -> 4; matrix products, arithmetic and copies ran while one was open for 14% -> 1% of each run, Pallas kernels for 0% -> 5%
where the time goes in v2:
time: 106 us; the launch traced here: 105 us
  starting transfers between devices  76.9 us (73%)
  waiting for transfers between devices  13.3 us (13%)
  Pallas kernels  10.3 us (10%)
  between operations  2.2 us (2%)
  local copies, waits for them, and re-layouts  1.93 us (2%)
    ppermute x9, starting transfers between devices, from_group(): lax.ppermute(block, 'dp', [((i + distance) % count, i) for i in range(cou...  57.1 us
    ppermute x5, starting transfers between devices, from_member(): return lax.ppermute(block, 'rows', [(i ^ flip, i) for i in range(MEMBERS)])  17.8 us
    ppermute x9, waiting for transfers between devices, from_group(): lax.ppermute(block, 'dp', [((i + distance) % count, i) for i in range(cou...  13.3 us
    pallas_call x5, Pallas kernels, kernel_call(): pl.pallas_call(body, out_shape=[jax.ShapeDtypeStruct(s, d) for s, d in ou...  10.3 us
  transfers between devices with their start and end apart: 15, of which 4 were waited for; matrix products, arithmetic and copies ran while one was open for 1% of the time, Pallas kernels for 5%

profile of v2, /device:TPU:1, one launch (start us, length us, event | category | flops | bytes accessed | tf_op | source)
XLA Modules:
  0.0 105.4 jit_solution(7139680077189522602)
XLA Ops:
  0.6 19.1 %collective-permute-start.4 = (bf16[128,1152]{1,0:T(8,128)(2,1)}, bf16[128,1152]{1,0:T(8,128)(2,1)S(1)}, u32[]{:S(2)}, u32[]{:S(2)}) collective-permute-start(bf16[128,1152]{1,0:T(8,128)(2,1)} %raw.3), channel_id=1, source_target_pairs={{12,0},{16,4},{20,8},{24,12},{28,16},{32,20},{36,24},{40,28},{44,3... | collective-permute-start | bytes 884744 | tf_op jit(solution)/shard_map/ppermute | solution.py:21
  19.7 3.1 %collective-permute-start.3 = (bf16[128,1152]{1,0:T(8,128)(2,1)}, bf16[128,1152]{1,0:T(8,128)(2,1)S(1)}, u32[]{:S(2)}, u32[]{:S(2)}) collective-permute-start(bf16[128,1152]{1,0:T(8,128)(2,1)} %raw.3), channel_id=1, source_target_pairs={{764,0},{0,4},{4,8},{8,12},{12,16},{16,20},{20,24},{24,28},{28,32}... | collective-permute-start | bytes 884744 | tf_op jit(solution)/shard_map/ppermute | solution.py:21
  22.9 4.8 %collective-permute-start.1 = (bf16[128,1152]{1,0:T(8,128)(2,1)}, bf16[128,1152]{1,0:T(8,128)(2,1)S(1)}, u32[]{:S(2)}, u32[]{:S(2)}) collective-permute-start(bf16[128,1152]{1,0:T(8,128)(2,1)} %raw.2), channel_id=1, source_target_pairs={{2,0},{3,1},{0,2},{1,3},{6,4},{7,5},{4,6},{5,7},{10,8},{11,9},{8,1... | collective-permute-start | bytes 884744 | tf_op jit(solution)/shard_map/ppermute | solution.py:16
  27.6 3.4 %collective-permute-start = (bf16[128,1152]{1,0:T(8,128)(2,1)}, bf16[128,1152]{1,0:T(8,128)(2,1)S(1)}, u32[]{:S(2)}, u32[]{:S(2)}) collective-permute-start(bf16[128,1152]{1,0:T(8,128)(2,1)} %raw.2), channel_id=1, source_target_pairs={{1,0},{0,1},{3,2},{2,3},{5,4},{4,5},{7,6},{6,7},{9,8},{8,9},{11,10... | collective-permute-start | bytes 884744 | tf_op jit(solution)/shard_map/ppermute | solution.py:16
  31.1 8.2 %collective-permute-start.7 = (bf16[128,1152]{1,0:T(8,128)(2,1)}, bf16[128,1152]{1,0:T(8,128)(2,1)S(1)}, u32[]{:S(2)}, u32[]{:S(2)}) collective-permute-start(bf16[128,1152]{1,0:T(8,128)(2,1)} %raw.3), channel_id=1, source_target_pairs={{4,0},{8,4},{12,8},{16,12},{20,16},{24,20},{28,24},{32,28},{36,32}... | collective-permute-start | bytes 884744 | tf_op jit(solution)/shard_map/ppermute | solution.py:21
  40.6 0.0 collective-permute-done.4.third
  40.6 0.0 collective-permute-done.3.behind
  40.7 1.9 %collective-permute-start.5 = (bf16[128,1152]{1,0:T(8,128)(2,1)S(1)}, bf16[128,1152]{1,0:T(8,128)(2,1)S(1)}, u32[]{:S(2)}, u32[]{:S(2)}) collective-permute-start(bf16[128,1152]{1,0:T(8,128)(2,1)S(1)} %broadcast_select_fusion), channel_id=1, source_target_pairs={{12,0},{0,4},{4,8},{8,12},{28,16},{16,20},{20,24},{24,28},{44,32},... | collective-permute-start | bytes 884744 | tf_op jit(solution)/shard_map/ppermute | solution.py:142
  42.6 1.9 %collective-permute-start.6 = (bf16[128,1152]{1,0:T(8,128)(2,1)S(1)}, bf16[128,1152]{1,0:T(8,128)(2,1)S(1)}, u32[]{:S(2)}, u32[]{:S(2)}) collective-permute-start(bf16[128,1152]{1,0:T(8,128)(2,1)S(1)} %collective-permute-done.3.behind), channel_id=1, source_target_pairs={{764,0},{0,4},{4,8},{8,12},{12,16},{16,20},{20,24},{24,28},{28,32}... | collective-permute-start | bytes 884744 | tf_op jit(solution)/shard_map/ppermute | solution.py:21
  44.5 0.0 collective-permute-done.1.c
  44.5 2.2 %collective-permute-start.2 = (bf16[128,1152]{1,0:T(8,128)(2,1)S(1)}, bf16[128,1152]{1,0:T(8,128)(2,1)S(1)}, u32[]{:S(2)}, u32[]{:S(2)}) collective-permute-start(bf16[128,1152]{1,0:T(8,128)(2,1)S(1)} %collective-permute-done.1.c), channel_id=1, source_target_pairs={{1,0},{0,1},{3,2},{2,3},{5,4},{4,5},{7,6},{6,7},{9,8},{8,9},{11,10... | collective-permute-start | bytes 884744 | tf_op jit(solution)/shard_map/ppermute | solution.py:16
  46.8 0.1 pad_maximum_fusion.scalars
  46.8 0.7 add_bitcast_fusion.target
  47.5 0.0 collective-permute-done.b
  47.5 0.5 collective-permute-done.7.ahead
  48.0 0.0 collective-permute-done.2.d
  48.0 0.0 copy-start
  48.0 1.0 copy-done
  49.0 0.0 copy-start.2
  49.0 1.0 copy-done.2
  49.9 3.6 %shard_map.68 = (f32[512,1152]{1,0:T(8,128)S(1)}, f32[128,1152]{1,0:T(8,128)S(1)}, bf16[128,1152]{1,0:T(8,128)(2,1)S(1)}, bf16[128,1152]{1,0:T(8,128)(2,1)S(1)}, bf16[128,1152]{1,0:T(8,128)(2,1)S(1)}) custom-call(f32[2]{0:T(128)S(1)} %pad_maximum_fusion.scalars, bf16[128,1152]{1,0:T(8,128)(2,1)S(1)} %copy-done, ...), custom_call_target="tpu_custom_call" | custom-call | tf_op jit(solution)/shard_map/pallas_call | solution.py:25
  53.5 0.0 collective-permute-done.5.ahead
  53.5 5.3 %collective-permute-done.6.behind = bf16[128,1152]{1,0:T(8,128)(2,1)S(1)} collective-permute-done((bf16[128,1152]{1,0:T(8,128)(2,1)S(1)}, bf16[128,1152]{1,0:T(8,128)(2,1)S(1)}, u32[]{:S(2)}, u32[]{:S(2)}) %collective-permute-start.6) | collective-permute-done | bytes 294944 | tf_op jit(solution)/shard_map/ppermute | solution.py:21
  58.8 0.0 copy-start.3
  58.8 3.2 %shard_map.69 = (bf16[2,128,1152]{2,1,0:T(8,128)(2,1)S(1)}, f32[2,128,1152]{2,1,0:T(8,128)S(1)}, bf16[128,1152]{1,0:T(8,128)(2,1)S(1)}, bf16[128,1152]{1,0:T(8,128)(2,1)S(1)}) custom-call(f32[2]{0:T(128)S(1)} %pad_maximum_fusion.scalars, bf16[128,1152]{1,0:T(8,128)(2,1)S(1)} %copy-done, bf16[128,1152]{1,0:T(8,128)(2,1)S(1)} %collective-permute-done.b, ...), custom_call_target="tpu_custom_call" | custom-call | tf_op jit(solution)/shard_map/pallas_call | solution.py:25
  62.1 3.0 %collective-permute-start.8 = (bf16[2,128,1152]{2,1,0:T(8,128)(2,1)S(1)}, bf16[2,128,1152]{2,1,0:T(8,128)(2,1)S(1)}, u32[]{:S(2)}, u32[]{:S(2)}) collective-permute-start(bf16[2,128,1152]{2,1,0:T(8,128)(2,1)S(1)} %get-tuple-element.15), channel_id=1, source_target_pairs={{1,0},{0,1},{3,2},{2,3},{5,4},{4,5},{7,6},{6,7},{9,8},{8,9},{11,10... | collective-permute-start | bytes 1769480 | tf_op jit(solution)/shard_map/ppermute | solution.py:16
  65.1 1.9 %collective-permute-start.13 = (bf16[128,1152]{1,0:T(8,128)(2,1)S(1)}, bf16[128,1152]{1,0:T(8,128)(2,1)S(1)}, u32[]{:S(2)}, u32[]{:S(2)}) collective-permute-start(bf16[128,1152]{1,0:T(8,128)(2,1)S(1)} %get-tuple-element.22), channel_id=1, source_target_pairs={{760,0},{764,4},{0,8},{4,12},{8,16},{12,20},{16,24},{20,28},{24,32... | collective-permute-start | bytes 884744 | tf_op jit(solution)/shard_map/ppermute | solution.py:21
  67.0 9.7 %collective-permute-start.14 = (bf16[128,1152]{1,0:T(8,128)(2,1)S(1)}, bf16[128,1152]{1,0:T(8,128)(2,1)S(1)}, u32[]{:S(2)}, u32[]{:S(2)}) collective-permute-start(bf16[128,1152]{1,0:T(8,128)(2,1)S(1)} %get-tuple-element.23), channel_id=1, source_target_pairs={{8,0},{12,4},{16,8},{20,12},{24,16},{28,20},{32,24},{36,28},{40,32... | collective-permute-start | bytes 884744 | tf_op jit(solution)/shard_map/ppermute | solution.py:21
  76.7 1.9 %collective-permute-start.10 = (bf16[128,1152]{1,0:T(8,128)(2,1)S(1)}, bf16[128,1152]{1,0:T(8,128)(2,1)S(1)}, u32[]{:S(2)}, u32[]{:S(2)}) collective-permute-start(bf16[128,1152]{1,0:T(8,128)(2,1)S(1)} %get-tuple-element.19), channel_id=1, source_target_pairs={{764,0},{0,4},{4,8},{8,12},{12,16},{16,20},{20,24},{24,28},{28,32}... | collective-permute-start | bytes 884744 | tf_op jit(solution)/shard_map/ppermute | solution.py:21
  78.6 9.4 %collective-permute-start.11 = (bf16[128,1152]{1,0:T(8,128)(2,1)S(1)}, bf16[128,1152]{1,0:T(8,128)(2,1)S(1)}, u32[]{:S(2)}, u32[]{:S(2)}) collective-permute-start(bf16[128,1152]{1,0:T(8,128)(2,1)S(1)} %get-tuple-element.20), channel_id=1, source_target_pairs={{4,0},{8,4},{12,8},{16,12},{20,16},{24,20},{28,24},{32,28},{36,32}... | collective-permute-start | bytes 884744 | tf_op jit(solution)/shard_map/ppermute | solution.py:21
  88.0 0.0 collective-permute-done.8.near
  88.0 1.9 %collective-permute-start.12 = (bf16[128,1152]{1,0:T(8,128)(2,1)S(1)}, bf16[128,1152]{1,0:T(8,128)(2,1)S(1)}, u32[]{:S(2)}, u32[]{:S(2)}) collective-permute-start(bf16[128,1152]{1,0:T(8,128)(2,1)S(1)} %get-tuple-element.21), channel_id=1, source_target_pairs={{756,0},{760,4},{764,8},{0,12},{4,16},{8,20},{12,24},{16,28},{20,3... | collective-permute-start | bytes 884744 | tf_op jit(solution)/shard_map/ppermute | solution.py:21
  89.9 0.0 copy-start.1
  90.0 0.1 shard_map.70
  90.1 0.0 collective-permute-done.13.parts_3_
  90.1 4.4 %collective-permute-start.9 = (bf16[128,1152]{1,0:T(8,128)(2,1)S(1)}, bf16[128,1152]{1,0:T(8,128)(2,1)S(1)}, u32[]{:S(2)}, u32[]{:S(2)}) collective-permute-start(bf16[128,1152]{1,0:T(8,128)(2,1)S(1)} %get-tuple-element.17), channel_id=1, source_target_pairs={{2,0},{3,1},{0,2},{1,3},{6,4},{7,5},{4,6},{5,7},{10,8},{11,9},{8,1... | collective-permute-start | bytes 884744 | tf_op jit(solution)/shard_map/ppermute | solution.py:16
  94.6 0.0 collective-permute-done.14.parts_4_
  94.6 0.0 collective-permute-done.10.parts_0_
  94.6 1.7 %collective-permute-done.11.parts_1_ = bf16[128,1152]{1,0:T(8,128)(2,1)S(1)} collective-permute-done((bf16[128,1152]{1,0:T(8,128)(2,1)S(1)}, bf16[128,1152]{1,0:T(8,128)(2,1)S(1)}, u32[]{:S(2)}, u32[]{:S(2)}) %collective-permute-start.11) | collective-permute-done | bytes 294944 | tf_op jit(solution)/shard_map/ppermute | solution.py:21
  96.3 5.8 %collective-permute-done.12.parts_2_ = bf16[128,1152]{1,0:T(8,128)(2,1)S(1)} collective-permute-done((bf16[128,1152]{1,0:T(8,128)(2,1)S(1)}, bf16[128,1152]{1,0:T(8,128)(2,1)S(1)}, u32[]{:S(2)}, u32[]{:S(2)}) %collective-permute-start.12) | collective-permute-done | bytes 294944 | tf_op jit(solution)/shard_map/ppermute | solution.py:21
  102.1 0.0 copy-done.3
  102.1 1.8 %shard_map.72 = f32[128,1152]{1,0:T(8,128)} custom-call(f32[2]{0:T(128)S(1)} %pad_maximum_fusion.scalars, bf16[128,1152]{1,0:T(8,128)(2,1)S(1)} %copy-done.3, f32[128,1152]{1,0:T(8,128)S(1)} %get-tuple-element.18.mine, bf16[128,1152]{1,0:T(8,128)(2,1)S(1)} %collective-permute-done.10.parts_0_, bf16[128,1152]{1,0:T(8,128)(2,1)S(1)} %collective-permute-done.11.parts_1_, ...), custom_call_target="tpu_custom_call" | custom-call | tf_op jit(solution)/shard_map/pallas_call | solution.py:25
  103.9 0.0 collective-permute-done.9.far
  103.9 0.0 copy-done.1
  103.9 1.5 %shard_map.71 = f32[128,1152]{1,0:T(8,128)} custom-call(f32[2]{0:T(128)S(1)} %pad_maximum_fusion.scalars, bf16[128,1152]{1,0:T(8,128)(2,1)S(1)} %copy-done.1, f32[128,1152]{1,0:T(8,128)S(1)} %get-tuple-element.16.own, bf16[128,1152]{1,0:T(8,128)(2,1)S(1)} %collective-permute-done.9.far), custom_call_target="tpu_custom_call" | custom-call | tf_op jit(solution)/shard_map/pallas_call | solution.py:25
  (1 shorter events, 0.0 us)
Async XLA Ops:
  0.6 40.0 %collective-permute-start.4 = (bf16[128,1152]{1,0:T(8,128)(2,1)}, bf16[128,1152]{1,0:T(8,128)(2,1)S(1)}, u32[]{:S(2)}, u32[]{:S(2)}) collective-permute-start(bf16[128,1152]{1,0:T(8,128)(2,1)} %raw.3), channel_id=1, source_target_pairs={{12,0},{16,4},{20,8},{24,12},{28,16},{32,20},{36,24},{40,28},{44,3... | collective-permute-start | bytes 884744 | tf_op jit(solution)/shard_map/ppermute | solution.py:21
  19.7 20.9 %collective-permute-start.3 = (bf16[128,1152]{1,0:T(8,128)(2,1)}, bf16[128,1152]{1,0:T(8,128)(2,1)S(1)}, u32[]{:S(2)}, u32[]{:S(2)}) collective-permute-start(bf16[128,1152]{1,0:T(8,128)(2,1)} %raw.3), channel_id=1, source_target_pairs={{764,0},{0,4},{4,8},{8,12},{12,16},{16,20},{20,24},{24,28},{28,32}... | collective-permute-start | bytes 884744 | tf_op jit(solution)/shard_map/ppermute | solution.py:21
  22.9 21.7 %collective-permute-start.1 = (bf16[128,1152]{1,0:T(8,128)(2,1)}, bf16[128,1152]{1,0:T(8,128)(2,1)S(1)}, u32[]{:S(2)}, u32[]{:S(2)}) collective-permute-start(bf16[128,1152]{1,0:T(8,128)(2,1)} %raw.2), channel_id=1, source_target_pairs={{2,0},{3,1},{0,2},{1,3},{6,4},{7,5},{4,6},{5,7},{10,8},{11,9},{8,1... | collective-permute-start | bytes 884744 | tf_op jit(solution)/shard_map/ppermute | solution.py:16
  27.6 19.9 %collective-permute-start = (bf16[128,1152]{1,0:T(8,128)(2,1)}, bf16[128,1152]{1,0:T(8,128)(2,1)S(1)}, u32[]{:S(2)}, u32[]{:S(2)}) collective-permute-start(bf16[128,1152]{1,0:T(8,128)(2,1)} %raw.2), channel_id=1, source_target_pairs={{1,0},{0,1},{3,2},{2,3},{5,4},{4,5},{7,6},{6,7},{9,8},{8,9},{11,10... | collective-permute-start | bytes 884744 | tf_op jit(solution)/shard_map/ppermute | solution.py:16
  31.1 16.9 %collective-permute-start.7 = (bf16[128,1152]{1,0:T(8,128)(2,1)}, bf16[128,1152]{1,0:T(8,128)(2,1)S(1)}, u32[]{:S(2)}, u32[]{:S(2)}) collective-permute-start(bf16[128,1152]{1,0:T(8,128)(2,1)} %raw.3), channel_id=1, source_target_pairs={{4,0},{8,4},{12,8},{16,12},{20,16},{24,20},{28,24},{32,28},{36,32}... | collective-permute-start | bytes 884744 | tf_op jit(solution)/shard_map/ppermute | solution.py:21
  40.7 12.9 %collective-permute-start.5 = (bf16[128,1152]{1,0:T(8,128)(2,1)S(1)}, bf16[128,1152]{1,0:T(8,128)(2,1)S(1)}, u32[]{:S(2)}, u32[]{:S(2)}) collective-permute-start(bf16[128,1152]{1,0:T(8,128)(2,1)S(1)} %broadcast_select_fusion), channel_id=1, source_target_pairs={{12,0},{0,4},{4,8},{8,12},{28,16},{16,20},{20,24},{24,28},{44,32},... | collective-permute-start | bytes 884744 | tf_op jit(solution)/shard_map/ppermute | solution.py:142
  42.6 16.2 %collective-permute-start.6 = (bf16[128,1152]{1,0:T(8,128)(2,1)S(1)}, bf16[128,1152]{1,0:T(8,128)(2,1)S(1)}, u32[]{:S(2)}, u32[]{:S(2)}) collective-permute-start(bf16[128,1152]{1,0:T(8,128)(2,1)S(1)} %collective-permute-done.3.behind), channel_id=1, source_target_pairs={{764,0},{0,4},{4,8},{8,12},{12,16},{16,20},{20,24},{24,28},{28,32}... | collective-permute-start | bytes 884744 | tf_op jit(solution)/shard_map/ppermute | solution.py:21
  44.5 3.5 %collective-permute-start.2 = (bf16[128,1152]{1,0:T(8,128)(2,1)S(1)}, bf16[128,1152]{1,0:T(8,128)(2,1)S(1)}, u32[]{:S(2)}, u32[]{:S(2)}) collective-permute-start(bf16[128,1152]{1,0:T(8,128)(2,1)S(1)} %collective-permute-done.1.c), channel_id=1, source_target_pairs={{1,0},{0,1},{3,2},{2,3},{5,4},{4,5},{7,6},{6,7},{9,8},{8,9},{11,10... | collective-permute-start | bytes 884744 | tf_op jit(solution)/shard_map/ppermute | solution.py:16
  48.0 1.0 copy-start
  49.0 1.0 copy-start.2
  58.8 43.3 %copy-start.3 = (bf16[128,1152]{1,0:T(8,128)(2,1)S(1)}, bf16[128,1152]{1,0:T(8,128)(2,1)}, u32[]{:S(2)}) copy-start(bf16[128,1152]{1,0:T(8,128)(2,1)} %raw.3) | copy-start | bytes 884740
  62.1 26.0 %collective-permute-start.8 = (bf16[2,128,1152]{2,1,0:T(8,128)(2,1)S(1)}, bf16[2,128,1152]{2,1,0:T(8,128)(2,1)S(1)}, u32[]{:S(2)}, u32[]{:S(2)}) collective-permute-start(bf16[2,128,1152]{2,1,0:T(8,128)(2,1)S(1)} %get-tuple-element.15), channel_id=1, source_target_pairs={{1,0},{0,1},{3,2},{2,3},{5,4},{4,5},{7,6},{6,7},{9,8},{8,9},{11,10... | collective-permute-start | bytes 1769480 | tf_op jit(solution)/shard_map/ppermute | solution.py:16
  65.1 25.0 %collective-permute-start.13 = (bf16[128,1152]{1,0:T(8,128)(2,1)S(1)}, bf16[128,1152]{1,0:T(8,128)(2,1)S(1)}, u32[]{:S(2)}, u32[]{:S(2)}) collective-permute-start(bf16[128,1152]{1,0:T(8,128)(2,1)S(1)} %get-tuple-element.22), channel_id=1, source_target_pairs={{760,0},{764,4},{0,8},{4,12},{8,16},{12,20},{16,24},{20,28},{24,32... | collective-permute-start | bytes 884744 | tf_op jit(solution)/shard_map/ppermute | solution.py:21
  67.0 27.6 %collective-permute-start.14 = (bf16[128,1152]{1,0:T(8,128)(2,1)S(1)}, bf16[128,1152]{1,0:T(8,128)(2,1)S(1)}, u32[]{:S(2)}, u32[]{:S(2)}) collective-permute-start(bf16[128,1152]{1,0:T(8,128)(2,1)S(1)} %get-tuple-element.23), channel_id=1, source_target_pairs={{8,0},{12,4},{16,8},{20,12},{24,16},{28,20},{32,24},{36,28},{40,32... | collective-permute-start | bytes 884744 | tf_op jit(solution)/shard_map/ppermute | solution.py:21
  76.7 17.9 %collective-permute-start.10 = (bf16[128,1152]{1,0:T(8,128)(2,1)S(1)}, bf16[128,1152]{1,0:T(8,128)(2,1)S(1)}, u32[]{:S(2)}, u32[]{:S(2)}) collective-permute-start(bf16[128,1152]{1,0:T(8,128)(2,1)S(1)} %get-tuple-element.19), channel_id=1, source_target_pairs={{764,0},{0,4},{4,8},{8,12},{12,16},{16,20},{20,24},{24,28},{28,32}... | collective-permute-start | bytes 884744 | tf_op jit(solution)/shard_map/ppermute | solution.py:21
  78.6 17.7 %collective-permute-start.11 = (bf16[128,1152]{1,0:T(8,128)(2,1)S(1)}, bf16[128,1152]{1,0:T(8,128)(2,1)S(1)}, u32[]{:S(2)}, u32[]{:S(2)}) collective-permute-start(bf16[128,1152]{1,0:T(8,128)(2,1)S(1)} %get-tuple-element.20), channel_id=1, source_target_pairs={{4,0},{8,4},{12,8},{16,12},{20,16},{24,20},{28,24},{32,28},{36,32}... | collective-permute-start | bytes 884744 | tf_op jit(solution)/shard_map/ppermute | solution.py:21
  88.0 14.1 %collective-permute-start.12 = (bf16[128,1152]{1,0:T(8,128)(2,1)S(1)}, bf16[128,1152]{1,0:T(8,128)(2,1)S(1)}, u32[]{:S(2)}, u32[]{:S(2)}) collective-permute-start(bf16[128,1152]{1,0:T(8,128)(2,1)S(1)} %get-tuple-element.21), channel_id=1, source_target_pairs={{756,0},{760,4},{764,8},{0,12},{4,16},{8,20},{12,24},{16,28},{20,3... | collective-permute-start | bytes 884744 | tf_op jit(solution)/shard_map/ppermute | solution.py:21
  89.9 14.0 %copy-start.1 = (bf16[128,1152]{1,0:T(8,128)(2,1)S(1)}, bf16[128,1152]{1,0:T(8,128)(2,1)}, u32[]{:S(2)}) copy-start(bf16[128,1152]{1,0:T(8,128)(2,1)} %raw.2) | copy-start | bytes 884740
  90.1 13.8 %collective-permute-start.9 = (bf16[128,1152]{1,0:T(8,128)(2,1)S(1)}, bf16[128,1152]{1,0:T(8,128)(2,1)S(1)}, u32[]{:S(2)}, u32[]{:S(2)}) collective-permute-start(bf16[128,1152]{1,0:T(8,128)(2,1)S(1)} %get-tuple-element.17), channel_id=1, source_target_pairs={{2,0},{3,1},{0,2},{1,3},{6,4},{7,5},{4,6},{5,7},{10,8},{11,9},{8,1... | collective-permute-start | bytes 884744 | tf_op jit(solution)/shard_map/ppermute | solution.py:16

commit v3 on v2

--- a/solution.py
+++ b/solution.py
@@ -57,7 +57,7 @@
     own = []
     for i, offset in enumerate(offsets):
         block = logits[:quarter, i * quarter : (i + 1) * quarter]
-        sign = jnp.where(jnp.logical_and(diagonal, target == offset), -1.0, 1.0)
+        sign = jnp.where(jnp.logical_and(diagonal, target == offset + 2), -1.0, 1.0)
         own.append(sign * sigmoid(sign * block))
     own = jnp.concatenate(own, axis=1).astype(LOW)
     weights = jnp.concatenate([own, sigmoid(logits[quarter:]).astype(LOW)])
@@ -128,7 +128,7 @@
     shard, two, four = (quarter, width), (2 * quarter, width), (MEMBERS * quarter, width)
     count = lax.axis_size("dp")
     scalars = jnp.concatenate([jnp.exp(logit_log_scale), bias])
-    target = (positive_offset - 2).reshape(1, quarter)
+    target = positive_offset.reshape(1, quarter)
 
     images_far = from_member(images, 2)
     text = {0: texts}

time: 106 us -> 111 us (1.047)
  the two profiles are of different devices: /device:TPU:1 before, /device:TPU:59 now
where the time goes in v3:
time: 111 us; the launch traced here: 110 us
  starting transfers between devices  68.4 us (62%)
  waiting for transfers between devices  26.4 us (24%)
  Pallas kernels  10.3 us (9%)
  local copies, waits for them, and re-layouts  2.58 us (2%)
  between operations  2.2 us (2%)
    ppermute x9, starting transfers between devices, from_group(): lax.ppermute(block, 'dp', [((i + distance) % count, i) for i in range(cou...  49.2 us
    ppermute x5, waiting for transfers between devices, from_member(): return lax.ppermute(block, 'rows', [(i ^ flip, i) for i in range(MEMBERS)])  18.1 us
    ppermute x5, starting transfers between devices, from_member(): return lax.ppermute(block, 'rows', [(i ^ flip, i) for i in range(MEMBERS)])  16.1 us
    pallas_call x5, Pallas kernels, kernel_call(): pl.pallas_call(body, out_shape=[jax.ShapeDtypeStruct(s, d) for s, d in ou...  10.3 us
    ppermute x9, waiting for transfers between devices, from_group(): lax.ppermute(block, 'dp', [((i + distance) % count, i) for i in range(cou...  8.26 us
    ppermute x1, starting transfers between devices, local(): lax.ppermute(jnp.where(column == 3, text[-1], text[3]), 'dp', line)  3.09 us
    unnamed x10, local copies, waits for them, and re-layouts  2.58 us
  transfers between devices with their start and end apart: 15, of which 5 were waited for; matrix products, arithmetic and copies ran while one was open for 0% of the time, Pallas kernels for 5%

profile of v3, /device:TPU:59, one launch (start us, length us, event | category | flops | bytes accessed | tf_op | source)
XLA Modules:
  0.0 110.0 jit_solution(17090178271230813137)
XLA Ops:
  0.6 4.4 %collective-permute-start.1 = (bf16[128,1152]{1,0:T(8,128)(2,1)}, bf16[128,1152]{1,0:T(8,128)(2,1)S(1)}, u32[]{:S(2)}, u32[]{:S(2)}) collective-permute-start(bf16[128,1152]{1,0:T(8,128)(2,1)} %raw.2), channel_id=1, source_target_pairs={{2,0},{3,1},{0,2},{1,3},{6,4},{7,5},{4,6},{5,7},{10,8},{11,9},{8,1... | collective-permute-start | bytes 884744 | tf_op jit(solution)/shard_map/ppermute | solution.py:16
  5.1 3.0 %collective-permute-start.4 = (bf16[128,1152]{1,0:T(8,128)(2,1)}, bf16[128,1152]{1,0:T(8,128)(2,1)S(1)}, u32[]{:S(2)}, u32[]{:S(2)}) collective-permute-start(bf16[128,1152]{1,0:T(8,128)(2,1)} %raw.3), channel_id=1, source_target_pairs={{12,0},{16,4},{20,8},{24,12},{28,16},{32,20},{36,24},{40,28},{44,3... | collective-permute-start | bytes 884744 | tf_op jit(solution)/shard_map/ppermute | solution.py:21
  8.1 2.8 %collective-permute-start.3 = (bf16[128,1152]{1,0:T(8,128)(2,1)}, bf16[128,1152]{1,0:T(8,128)(2,1)S(1)}, u32[]{:S(2)}, u32[]{:S(2)}) collective-permute-start(bf16[128,1152]{1,0:T(8,128)(2,1)} %raw.3), channel_id=1, source_target_pairs={{764,0},{0,4},{4,8},{8,12},{12,16},{16,20},{20,24},{24,28},{28,32}... | collective-permute-start | bytes 884744 | tf_op jit(solution)/shard_map/ppermute | solution.py:21
  10.9 3.4 %collective-permute-start = (bf16[128,1152]{1,0:T(8,128)(2,1)}, bf16[128,1152]{1,0:T(8,128)(2,1)S(1)}, u32[]{:S(2)}, u32[]{:S(2)}) collective-permute-start(bf16[128,1152]{1,0:T(8,128)(2,1)} %raw.2), channel_id=1, source_target_pairs={{1,0},{0,1},{3,2},{2,3},{5,4},{4,5},{7,6},{6,7},{9,8},{8,9},{11,10... | collective-permute-start | bytes 884744 | tf_op jit(solution)/shard_map/ppermute | solution.py:16
  14.4 2.5 %collective-permute-start.7 = (bf16[128,1152]{1,0:T(8,128)(2,1)}, bf16[128,1152]{1,0:T(8,128)(2,1)S(1)}, u32[]{:S(2)}, u32[]{:S(2)}) collective-permute-start(bf16[128,1152]{1,0:T(8,128)(2,1)} %raw.3), channel_id=1, source_target_pairs={{4,0},{8,4},{12,8},{16,12},{20,16},{24,20},{28,24},{32,28},{36,32}... | collective-permute-start | bytes 884744 | tf_op jit(solution)/shard_map/ppermute | solution.py:21
  16.8 4.5 %collective-permute-done.1.c = bf16[128,1152]{1,0:T(8,128)(2,1)S(1)} collective-permute-done((bf16[128,1152]{1,0:T(8,128)(2,1)}, bf16[128,1152]{1,0:T(8,128)(2,1)S(1)}, u32[]{:S(2)}, u32[]{:S(2)}) %collective-permute-start.1) | collective-permute-done | bytes 294944 | tf_op jit(solution)/shard_map/ppermute | solution.py:16
  21.3 3.4 %collective-permute-start.2 = (bf16[128,1152]{1,0:T(8,128)(2,1)S(1)}, bf16[128,1152]{1,0:T(8,128)(2,1)S(1)}, u32[]{:S(2)}, u32[]{:S(2)}) collective-permute-start(bf16[128,1152]{1,0:T(8,128)(2,1)S(1)} %collective-permute-done.1.c), channel_id=1, source_target_pairs={{1,0},{0,1},{3,2},{2,3},{5,4},{4,5},{7,6},{6,7},{9,8},{8,9},{11,10... | collective-permute-start | bytes 884744 | tf_op jit(solution)/shard_map/ppermute | solution.py:16
  24.7 0.0 collective-permute-done.4.third
  24.7 0.0 collective-permute-done.3.behind
  24.8 3.1 %collective-permute-start.5 = (bf16[128,1152]{1,0:T(8,128)(2,1)S(1)}, bf16[128,1152]{1,0:T(8,128)(2,1)S(1)}, u32[]{:S(2)}, u32[]{:S(2)}) collective-permute-start(bf16[128,1152]{1,0:T(8,128)(2,1)S(1)} %broadcast_select_fusion), channel_id=1, source_target_pairs={{12,0},{0,4},{4,8},{8,12},{28,16},{16,20},{20,24},{24,28},{44,32},... | collective-permute-start | bytes 884744 | tf_op jit(solution)/shard_map/ppermute | solution.py:142
  27.9 2.5 %collective-permute-start.6 = (bf16[128,1152]{1,0:T(8,128)(2,1)S(1)}, bf16[128,1152]{1,0:T(8,128)(2,1)S(1)}, u32[]{:S(2)}, u32[]{:S(2)}) collective-permute-start(bf16[128,1152]{1,0:T(8,128)(2,1)S(1)} %collective-permute-done.3.behind), channel_id=1, source_target_pairs={{764,0},{0,4},{4,8},{8,12},{12,16},{16,20},{20,24},{24,28},{28,32}... | collective-permute-start | bytes 884744 | tf_op jit(solution)/shard_map/ppermute | solution.py:21
  31.7 0.1 pad_maximum_fusion.scalars
  31.8 0.0 collective-permute-done.b
  31.8 0.0 collective-permute-done.7.ahead
  31.8 0.0 collective-permute-done.2.d
  31.8 0.0 copy-start
  31.8 1.0 copy-done
  32.8 0.0 copy-start.2
  32.8 1.0 copy-done.2
  33.7 0.0 copy-start.4
  33.7 0.7 copy-done.4
  34.4 3.6 %shard_map.68 = (f32[512,1152]{1,0:T(8,128)S(1)}, f32[128,1152]{1,0:T(8,128)S(1)}, bf16[128,1152]{1,0:T(8,128)(2,1)S(1)}, bf16[128,1152]{1,0:T(8,128)(2,1)S(1)}, bf16[128,1152]{1,0:T(8,128)(2,1)S(1)}) custom-call(f32[2]{0:T(128)S(1)} %pad_maximum_fusion.scalars, bf16[128,1152]{1,0:T(8,128)(2,1)S(1)} %copy-done, ...), custom_call_target="tpu_custom_call" | custom-call | tf_op jit(solution)/shard_map/pallas_call | solution.py:25
  38.0 0.0 collective-permute-done.5.ahead
  38.0 5.2 %collective-permute-done.6.behind = bf16[128,1152]{1,0:T(8,128)(2,1)S(1)} collective-permute-done((bf16[128,1152]{1,0:T(8,128)(2,1)S(1)}, bf16[128,1152]{1,0:T(8,128)(2,1)S(1)}, u32[]{:S(2)}, u32[]{:S(2)}) %collective-permute-start.6) | collective-permute-done | bytes 294944 | tf_op jit(solution)/shard_map/ppermute | solution.py:21
  43.1 0.0 copy-start.3
  43.1 3.2 %shard_map.69 = (bf16[2,128,1152]{2,1,0:T(8,128)(2,1)S(1)}, f32[2,128,1152]{2,1,0:T(8,128)S(1)}, bf16[128,1152]{1,0:T(8,128)(2,1)S(1)}, bf16[128,1152]{1,0:T(8,128)(2,1)S(1)}) custom-call(f32[2]{0:T(128)S(1)} %pad_maximum_fusion.scalars, bf16[128,1152]{1,0:T(8,128)(2,1)S(1)} %copy-done, bf16[128,1152]{1,0:T(8,128)(2,1)S(1)} %collective-permute-done.b, ...), custom_call_target="tpu_custom_call" | custom-call | tf_op jit(solution)/shard_map/pallas_call | solution.py:25
  46.4 2.9 %collective-permute-start.8 = (bf16[2,128,1152]{2,1,0:T(8,128)(2,1)S(1)}, bf16[2,128,1152]{2,1,0:T(8,128)(2,1)S(1)}, u32[]{:S(2)}, u32[]{:S(2)}) collective-permute-start(bf16[2,128,1152]{2,1,0:T(8,128)(2,1)S(1)} %get-tuple-element.15), channel_id=1, source_target_pairs={{1,0},{0,1},{3,2},{2,3},{5,4},{4,5},{7,6},{6,7},{9,8},{8,9},{11,10... | collective-permute-start | bytes 1769480 | tf_op jit(solution)/shard_map/ppermute | solution.py:16
  49.3 12.7 %collective-permute-start.13 = (bf16[128,1152]{1,0:T(8,128)(2,1)S(1)}, bf16[128,1152]{1,0:T(8,128)(2,1)S(1)}, u32[]{:S(2)}, u32[]{:S(2)}) collective-permute-start(bf16[128,1152]{1,0:T(8,128)(2,1)S(1)} %get-tuple-element.22), channel_id=1, source_target_pairs={{760,0},{764,4},{0,8},{4,12},{8,16},{12,20},{16,24},{20,28},{24,32... | collective-permute-start | bytes 884744 | tf_op jit(solution)/shard_map/ppermute | solution.py:21
  62.0 1.9 %collective-permute-start.14 = (bf16[128,1152]{1,0:T(8,128)(2,1)S(1)}, bf16[128,1152]{1,0:T(8,128)(2,1)S(1)}, u32[]{:S(2)}, u32[]{:S(2)}) collective-permute-start(bf16[128,1152]{1,0:T(8,128)(2,1)S(1)} %get-tuple-element.23), channel_id=1, source_target_pairs={{8,0},{12,4},{16,8},{20,12},{24,16},{28,20},{32,24},{36,28},{40,32... | collective-permute-start | bytes 884744 | tf_op jit(solution)/shard_map/ppermute | solution.py:21
  63.9 8.4 %collective-permute-start.10 = (bf16[128,1152]{1,0:T(8,128)(2,1)S(1)}, bf16[128,1152]{1,0:T(8,128)(2,1)S(1)}, u32[]{:S(2)}, u32[]{:S(2)}) collective-permute-start(bf16[128,1152]{1,0:T(8,128)(2,1)S(1)} %get-tuple-element.19), channel_id=1, source_target_pairs={{764,0},{0,4},{4,8},{8,12},{12,16},{16,20},{20,24},{24,28},{28,32}... | collective-permute-start | bytes 884744 | tf_op jit(solution)/shard_map/ppermute | solution.py:21
  72.3 1.9 %collective-permute-start.11 = (bf16[128,1152]{1,0:T(8,128)(2,1)S(1)}, bf16[128,1152]{1,0:T(8,128)(2,1)S(1)}, u32[]{:S(2)}, u32[]{:S(2)}) collective-permute-start(bf16[128,1152]{1,0:T(8,128)(2,1)S(1)} %get-tuple-element.20), channel_id=1, source_target_pairs={{4,0},{8,4},{12,8},{16,12},{20,16},{24,20},{28,24},{32,28},{36,32}... | collective-permute-start | bytes 884744 | tf_op jit(solution)/shard_map/ppermute | solution.py:21
  74.3 0.0 collective-permute-done.8.near
  74.3 13.5 %collective-permute-start.12 = (bf16[128,1152]{1,0:T(8,128)(2,1)S(1)}, bf16[128,1152]{1,0:T(8,128)(2,1)S(1)}, u32[]{:S(2)}, u32[]{:S(2)}) collective-permute-start(bf16[128,1152]{1,0:T(8,128)(2,1)S(1)} %get-tuple-element.21), channel_id=1, source_target_pairs={{756,0},{760,4},{764,8},{0,12},{4,16},{8,20},{12,24},{16,28},{20,3... | collective-permute-start | bytes 884744 | tf_op jit(solution)/shard_map/ppermute | solution.py:21
  87.8 0.0 copy-start.1
  87.8 0.1 shard_map.70
  88.0 0.0 collective-permute-done.13.parts_3_
  88.0 1.9 %collective-permute-start.9 = (bf16[128,1152]{1,0:T(8,128)(2,1)S(1)}, bf16[128,1152]{1,0:T(8,128)(2,1)S(1)}, u32[]{:S(2)}, u32[]{:S(2)}) collective-permute-start(bf16[128,1152]{1,0:T(8,128)(2,1)S(1)} %get-tuple-element.17), channel_id=1, source_target_pairs={{2,0},{3,1},{0,2},{1,3},{6,4},{7,5},{4,6},{5,7},{10,8},{11,9},{8,1... | collective-permute-start | bytes 884744 | tf_op jit(solution)/shard_map/ppermute | solution.py:16
  89.9 0.0 collective-permute-done.14.parts_4_
  89.9 0.0 collective-permute-done.10.parts_0_
  89.9 1.5 %collective-permute-done.11.parts_1_ = bf16[128,1152]{1,0:T(8,128)(2,1)S(1)} collective-permute-done((bf16[128,1152]{1,0:T(8,128)(2,1)S(1)}, bf16[128,1152]{1,0:T(8,128)(2,1)S(1)}, u32[]{:S(2)}, u32[]{:S(2)}) %collective-permute-start.11) | collective-permute-done | bytes 294944 | tf_op jit(solution)/shard_map/ppermute | solution.py:21
  91.4 1.5 %collective-permute-done.12.parts_2_ = bf16[128,1152]{1,0:T(8,128)(2,1)S(1)} collective-permute-done((bf16[128,1152]{1,0:T(8,128)(2,1)S(1)}, bf16[128,1152]{1,0:T(8,128)(2,1)S(1)}, u32[]{:S(2)}, u32[]{:S(2)}) %collective-permute-start.12) | collective-permute-done | bytes 294944 | tf_op jit(solution)/shard_map/ppermute | solution.py:21
  93.0 0.0 copy-done.3
  93.0 1.8 %shard_map.72 = f32[128,1152]{1,0:T(8,128)} custom-call(f32[2]{0:T(128)S(1)} %pad_maximum_fusion.scalars, bf16[128,1152]{1,0:T(8,128)(2,1)S(1)} %copy-done.3, f32[128,1152]{1,0:T(8,128)S(1)} %get-tuple-element.18.mine, bf16[128,1152]{1,0:T(8,128)(2,1)S(1)} %collective-permute-done.10.parts_0_, bf16[128,1152]{1,0:T(8,128)(2,1)S(1)} %collective-permute-done.11.parts_1_, ...), custom_call_target="tpu_custom_call" | custom-call | tf_op jit(solution)/shard_map/pallas_call | solution.py:25
  94.8 13.7 %collective-permute-done.9.far = bf16[128,1152]{1,0:T(8,128)(2,1)S(1)} collective-permute-done((bf16[128,1152]{1,0:T(8,128)(2,1)S(1)}, bf16[128,1152]{1,0:T(8,128)(2,1)S(1)}, u32[]{:S(2)}, u32[]{:S(2)}) %collective-permute-start.9) | collective-permute-done | bytes 294944 | tf_op jit(solution)/shard_map/ppermute | solution.py:16
  108.5 0.0 copy-done.1
  108.5 1.5 %shard_map.71 = f32[128,1152]{1,0:T(8,128)} custom-call(f32[2]{0:T(128)S(1)} %pad_maximum_fusion.scalars, bf16[128,1152]{1,0:T(8,128)(2,1)S(1)} %copy-done.1, f32[128,1152]{1,0:T(8,128)S(1)} %get-tuple-element.16.own, bf16[128,1152]{1,0:T(8,128)(2,1)S(1)} %collective-permute-done.9.far), custom_call_target="tpu_custom_call" | custom-call | tf_op jit(solution)/shard_map/pallas_call | solution.py:25
  (1 shorter events, 0.0 us)
Async XLA Ops:
  0.6 20.7 %collective-permute-start.1 = (bf16[128,1152]{1,0:T(8,128)(2,1)}, bf16[128,1152]{1,0:T(8,128)(2,1)S(1)}, u32[]{:S(2)}, u32[]{:S(2)}) collective-permute-start(bf16[128,1152]{1,0:T(8,128)(2,1)} %raw.2), channel_id=1, source_target_pairs={{2,0},{3,1},{0,2},{1,3},{6,4},{7,5},{4,6},{5,7},{10,8},{11,9},{8,1... | collective-permute-start | bytes 884744 | tf_op jit(solution)/shard_map/ppermute | solution.py:16
  5.1 19.6 %collective-permute-start.4 = (bf16[128,1152]{1,0:T(8,128)(2,1)}, bf16[128,1152]{1,0:T(8,128)(2,1)S(1)}, u32[]{:S(2)}, u32[]{:S(2)}) collective-permute-start(bf16[128,1152]{1,0:T(8,128)(2,1)} %raw.3), channel_id=1, source_target_pairs={{12,0},{16,4},{20,8},{24,12},{28,16},{32,20},{36,24},{40,28},{44,3... | collective-permute-start | bytes 884744 | tf_op jit(solution)/shard_map/ppermute | solution.py:21
  8.1 16.7 %collective-permute-start.3 = (bf16[128,1152]{1,0:T(8,128)(2,1)}, bf16[128,1152]{1,0:T(8,128)(2,1)S(1)}, u32[]{:S(2)}, u32[]{:S(2)}) collective-permute-start(bf16[128,1152]{1,0:T(8,128)(2,1)} %raw.3), channel_id=1, source_target_pairs={{764,0},{0,4},{4,8},{8,12},{12,16},{16,20},{20,24},{24,28},{28,32}... | collective-permute-start | bytes 884744 | tf_op jit(solution)/shard_map/ppermute | solution.py:21
  10.9 20.9 %collective-permute-start = (bf16[128,1152]{1,0:T(8,128)(2,1)}, bf16[128,1152]{1,0:T(8,128)(2,1)S(1)}, u32[]{:S(2)}, u32[]{:S(2)}) collective-permute-start(bf16[128,1152]{1,0:T(8,128)(2,1)} %raw.2), channel_id=1, source_target_pairs={{1,0},{0,1},{3,2},{2,3},{5,4},{4,5},{7,6},{6,7},{9,8},{8,9},{11,10... | collective-permute-start | bytes 884744 | tf_op jit(solution)/shard_map/ppermute | solution.py:16
  14.4 17.4 %collective-permute-start.7 = (bf16[128,1152]{1,0:T(8,128)(2,1)}, bf16[128,1152]{1,0:T(8,128)(2,1)S(1)}, u32[]{:S(2)}, u32[]{:S(2)}) collective-permute-start(bf16[128,1152]{1,0:T(8,128)(2,1)} %raw.3), channel_id=1, source_target_pairs={{4,0},{8,4},{12,8},{16,12},{20,16},{24,20},{28,24},{32,28},{36,32}... | collective-permute-start | bytes 884744 | tf_op jit(solution)/shard_map/ppermute | solution.py:21
  21.3 10.5 %collective-permute-start.2 = (bf16[128,1152]{1,0:T(8,128)(2,1)S(1)}, bf16[128,1152]{1,0:T(8,128)(2,1)S(1)}, u32[]{:S(2)}, u32[]{:S(2)}) collective-permute-start(bf16[128,1152]{1,0:T(8,128)(2,1)S(1)} %collective-permute-done.1.c), channel_id=1, source_target_pairs={{1,0},{0,1},{3,2},{2,3},{5,4},{4,5},{7,6},{6,7},{9,8},{8,9},{11,10... | collective-permute-start | bytes 884744 | tf_op jit(solution)/shard_map/ppermute | solution.py:16
  24.8 13.2 %collective-permute-start.5 = (bf16[128,1152]{1,0:T(8,128)(2,1)S(1)}, bf16[128,1152]{1,0:T(8,128)(2,1)S(1)}, u32[]{:S(2)}, u32[]{:S(2)}) collective-permute-start(bf16[128,1152]{1,0:T(8,128)(2,1)S(1)} %broadcast_select_fusion), channel_id=1, source_target_pairs={{12,0},{0,4},{4,8},{8,12},{28,16},{16,20},{20,24},{24,28},{44,32},... | collective-permute-start | bytes 884744 | tf_op jit(solution)/shard_map/ppermute | solution.py:142
  27.9 15.3 %collective-permute-start.6 = (bf16[128,1152]{1,0:T(8,128)(2,1)S(1)}, bf16[128,1152]{1,0:T(8,128)(2,1)S(1)}, u32[]{:S(2)}, u32[]{:S(2)}) collective-permute-start(bf16[128,1152]{1,0:T(8,128)(2,1)S(1)} %collective-permute-done.3.behind), channel_id=1, source_target_pairs={{764,0},{0,4},{4,8},{8,12},{12,16},{16,20},{20,24},{24,28},{28,32}... | collective-permute-start | bytes 884744 | tf_op jit(solution)/shard_map/ppermute | solution.py:21
  31.8 1.0 copy-start
  32.8 1.0 copy-start.2
  33.7 0.7 copy-start.4
  43.1 49.8 %copy-start.3 = (bf16[128,1152]{1,0:T(8,128)(2,1)S(1)}, bf16[128,1152]{1,0:T(8,128)(2,1)}, u32[]{:S(2)}) copy-start(bf16[128,1152]{1,0:T(8,128)(2,1)} %raw.3) | copy-start | bytes 884740
  46.4 27.9 %collective-permute-start.8 = (bf16[2,128,1152]{2,1,0:T(8,128)(2,1)S(1)}, bf16[2,128,1152]{2,1,0:T(8,128)(2,1)S(1)}, u32[]{:S(2)}, u32[]{:S(2)}) collective-permute-start(bf16[2,128,1152]{2,1,0:T(8,128)(2,1)S(1)} %get-tuple-element.15), channel_id=1, source_target_pairs={{1,0},{0,1},{3,2},{2,3},{5,4},{4,5},{7,6},{6,7},{9,8},{8,9},{11,10... | collective-permute-start | bytes 1769480 | tf_op jit(solution)/shard_map/ppermute | solution.py:16
  49.3 38.7 %collective-permute-start.13 = (bf16[128,1152]{1,0:T(8,128)(2,1)S(1)}, bf16[128,1152]{1,0:T(8,128)(2,1)S(1)}, u32[]{:S(2)}, u32[]{:S(2)}) collective-permute-start(bf16[128,1152]{1,0:T(8,128)(2,1)S(1)} %get-tuple-element.22), channel_id=1, source_target_pairs={{760,0},{764,4},{0,8},{4,12},{8,16},{12,20},{16,24},{20,28},{24,32... | collective-permute-start | bytes 884744 | tf_op jit(solution)/shard_map/ppermute | solution.py:21
  62.0 27.9 %collective-permute-start.14 = (bf16[128,1152]{1,0:T(8,128)(2,1)S(1)}, bf16[128,1152]{1,0:T(8,128)(2,1)S(1)}, u32[]{:S(2)}, u32[]{:S(2)}) collective-permute-start(bf16[128,1152]{1,0:T(8,128)(2,1)S(1)} %get-tuple-element.23), channel_id=1, source_target_pairs={{8,0},{12,4},{16,8},{20,12},{24,16},{28,20},{32,24},{36,28},{40,32... | collective-permute-start | bytes 884744 | tf_op jit(solution)/shard_map/ppermute | solution.py:21
  63.9 26.0 %collective-permute-start.10 = (bf16[128,1152]{1,0:T(8,128)(2,1)S(1)}, bf16[128,1152]{1,0:T(8,128)(2,1)S(1)}, u32[]{:S(2)}, u32[]{:S(2)}) collective-permute-start(bf16[128,1152]{1,0:T(8,128)(2,1)S(1)} %get-tuple-element.19), channel_id=1, source_target_pairs={{764,0},{0,4},{4,8},{8,12},{12,16},{16,20},{20,24},{24,28},{28,32}... | collective-permute-start | bytes 884744 | tf_op jit(solution)/shard_map/ppermute | solution.py:21
  72.3 19.1 %collective-permute-start.11 = (bf16[128,1152]{1,0:T(8,128)(2,1)S(1)}, bf16[128,1152]{1,0:T(8,128)(2,1)S(1)}, u32[]{:S(2)}, u32[]{:S(2)}) collective-permute-start(bf16[128,1152]{1,0:T(8,128)(2,1)S(1)} %get-tuple-element.20), channel_id=1, source_target_pairs={{4,0},{8,4},{12,8},{16,12},{20,16},{24,20},{28,24},{32,28},{36,32}... | collective-permute-start | bytes 884744 | tf_op jit(solution)/shard_map/ppermute | solution.py:21
  74.3 18.7 %collective-permute-start.12 = (bf16[128,1152]{1,0:T(8,128)(2,1)S(1)}, bf16[128,1152]{1,0:T(8,128)(2,1)S(1)}, u32[]{:S(2)}, u32[]{:S(2)}) collective-permute-start(bf16[128,1152]{1,0:T(8,128)(2,1)S(1)} %get-tuple-element.21), channel_id=1, source_target_pairs={{756,0},{760,4},{764,8},{0,12},{4,16},{8,20},{12,24},{16,28},{20,3... | collective-permute-start | bytes 884744 | tf_op jit(solution)/shard_map/ppermute | solution.py:21
  87.8 20.6 %copy-start.1 = (bf16[128,1152]{1,0:T(8,128)(2,1)S(1)}, bf16[128,1152]{1,0:T(8,128)(2,1)}, u32[]{:S(2)}) copy-start(bf16[128,1152]{1,0:T(8,128)(2,1)} %raw.2) | copy-start | bytes 884740
  88.0 20.5 %collective-permute-start.9 = (bf16[128,1152]{1,0:T(8,128)(2,1)S(1)}, bf16[128,1152]{1,0:T(8,128)(2,1)S(1)}, u32[]{:S(2)}, u32[]{:S(2)}) collective-permute-start(bf16[128,1152]{1,0:T(8,128)(2,1)S(1)} %get-tuple-element.17), channel_id=1, source_target_pairs={{2,0},{3,1},{0,2},{1,3},{6,4},{7,5},{4,6},{5,7},{10,8},{11,9},{8,1... | collective-permute-start | bytes 884744 | tf_op jit(solution)/shard_map/ppermute | solution.py:16
